TPU v7x, 128 devices: a whole 4x4x4 slice. The times are simulated.
128 devices in a mesh: grp: 4 (over z_lo, core), dev: 32 (over z_hi, x, y).
Axes of the slice: x: 4, y: 4, z: 4 (z_hi: 2, z_lo: 2; z = z_hi * 2 + z_lo), core: 2. Of those that a mesh axis runs over, the one named last changes fastest.
Arguments:
- pressure_old: float32 [128, 256, 256], P(('grp', 'dev')), may hold values from -6 to 6
- strain_change: float32 [128, 256, 256], P(('grp', 'dev')), may hold values from -3 to 3
- storage: float32 [128, 256, 256], P(('grp', 'dev')), may hold values from 0.05 to 0.5
- trans_x: float32 [128, 256, 256], P(('grp', 'dev')), may hold values from 0.3 to 3
- trans_y: float32 [128, 256, 256], P(('grp', 'dev')), may hold values from 0.3 to 3
- trans_z: float32 [128, 256, 256], P(('grp', 'dev')), may hold values from 0.3 to 3
- displacement_old: float32 [3, 128, 256, 256], P(None, 'grp', 'dev'), may hold values from -6 to 6
- modulus: float32 [128, 256, 256], P('grp', 'dev'), may hold values from 0.01 to 0.05
- perf_cell: int32 [512, 128], P(('grp', 'dev')), may hold values from 0 to 65535
- perf_well: int32 [512], P(('grp', 'dev')), may hold values from 0 to 255, as said below
- perf_count: int32 [512], P(('grp', 'dev')), may hold values from 1 to 128, as said below
- perf_index: float32 [512, 128], P(('grp', 'dev')), may hold values from 0.5 to 5
- well_rate: float32 [256], replicated, may hold values from -600 to 600
Outputs:
- pressure: float32 [128, 256, 256], P(('grp', 'dev'))
- displacement: float32 [3, 128, 256, 256], P(None, 'grp', 'dev')
- strain: float32 [128, 256, 256], P(('grp', 'dev'))
Inputs may be any that keep to these rules, and one draw needn't show every extreme that they name: `perf_well`: every well owns exactly two perforation blocks, which lie on devices drawn from the seed. `perf_count`: every draw has a block with all 128 rows live and a block with one live row.
All inputs are finite; a program needn't handle non-finite values.
Results may differ from a plain program's by a relative error of at most 0.0001.
Values sent between devices are 32-bit elements; how exact they have to be, the bound alone decides.
A program may use at most 64 MiB of HBM per device.

v0:
```python
import jax
import jax.numpy as jnp
from jax import lax
from jax.sharding import PartitionSpec as P

FLOW_SWEEPS = 4
MECH_SWEEPS = 6


biot_coeff = 0.8
relax_factor = 0.6
coupling_ratio = 1.5


def padded_2(block, sides, width):
    for axis, dim in sides:
        count = lax.axis_size(axis)
        forward = [(i, i + 1) for i in range(count - 1)]
        backward = [(target, source) for source, target in forward]
        low = lax.ppermute(
            lax.slice_in_dim(block, block.shape[dim] - width, None, axis=dim), axis, forward
        )
        high = lax.ppermute(lax.slice_in_dim(block, 0, width, axis=dim), axis, backward)
        block = jnp.concatenate([low, block, high], axis=dim)
    return block


def above_z(values):
    return jnp.concatenate([values[..., 1:], jnp.zeros_like(values[..., :1])], axis=-1)


def below_z(values):
    return jnp.concatenate([jnp.zeros_like(values[..., :1]), values[..., :-1]], axis=-1)


def gradients(field):
    grad_x = field[0, 2:, :] - field[0, :-2, :]
    grad_y = field[1, :, 2:] - field[1, :, :-2]
    grad_z = above_z(field[2]) - below_z(field[2])
    return (grad_x, grad_y, grad_z)


def stiffness(field):
    column_sum = field + above_z(field) + below_z(field)
    row_sum = column_sum[:, :, :-2] + column_sum[:, :, 1:-1] + column_sum[:, :, 2:]
    box_sum = row_sum[:, :-2] + row_sum[:, 1:-1] + row_sum[:, 2:]
    grad_x, grad_y, grad_z = gradients(field)
    along_x = grad_y + grad_z[:, 1:-1]
    along_y = grad_x + grad_z[1:-1]
    along_z = grad_x[:, 1:-1] + grad_y[1:-1]
    mixed_terms = jnp.stack(
        [
            along_x[2:] - along_x[:-2],
            along_y[:, 2:] - along_y[:, :-2],
            above_z(along_z) - below_z(along_z),
        ]
    )
    return 27.0 * field[:, 1:-1, 1:-1] - box_sum - 0.25 * coupling_ratio * mixed_terms


def divergence(field):
    grad_x, grad_y, grad_z = gradients(field)
    return 0.5 * (grad_x[:, 1:-1] + grad_y[1:-1] + grad_z[1:-1, 1:-1])


def forces(press):
    force_x = press[2:, 1:-1] - press[:-2, 1:-1]
    force_y = press[1:-1, 2:] - press[1:-1, :-2]
    middle = press[1:-1, 1:-1]
    force_z = above_z(middle) - below_z(middle)
    return -0.5 * biot_coeff * jnp.stack([force_x, force_y, force_z])


def trim_margin(values, amount):
    size_x = values.shape[-3]
    size_y = values.shape[-2]
    return values[..., amount : size_x - amount, amount : size_y - amount, :]


def flow_rim(values):
    return padded_2(values, ((("grp", "dev"), 0),), 1)


def mech_rim(values, width):
    return padded_2(values, (("grp", 1), ("dev", 2)), width)


def body(
    pressure_old,
    strain_change,
    storage,
    trans_x,
    trans_y,
    trans_z,
    displacement_old,
    modulus,
    perf_cell,
    perf_well,
    perf_count,
    perf_index,
    well_rate,
):
    rows_x = pressure_old.shape[0]
    cell_count = pressure_old.size
    block_rows = perf_cell.shape[1]
    well_count = well_rate.shape[0]
    last_device = lax.axis_index(("grp", "dev")) == lax.axis_size(("grp", "dev")) - 1
    edge_row = (jnp.arange(rows_x, dtype=jnp.int32) == rows_x - 1)[:, None, None]
    east_face = jnp.where(jnp.logical_and(last_device, edge_row), 0.0, trans_x)
    west_face = flow_rim(trans_x)[:-2]
    north_face = trans_y.at[:, -1].set(0.0)
    south_face = jnp.concatenate([jnp.zeros_like(trans_y[:, :1]), trans_y[:, :-1]], axis=1)
    upper_face = trans_z.at[:, :, -1].set(0.0)
    lower_face = jnp.concatenate([jnp.zeros_like(trans_z[:, :, :1]), trans_z[:, :, :-1]], axis=2)
    flat_cell = perf_cell.reshape(-1)
    live_rows = (jnp.arange(block_rows, dtype=jnp.int32)[None, :] < perf_count[:, None]).astype(
        jnp.float32
    )
    weight = perf_index * live_rows
    member = (perf_well[:, None] == jnp.arange(well_count, dtype=jnp.int32)[None, :]).astype(
        jnp.float32
    )
    strength_part = jnp.sum(member * jnp.sum(weight, axis=1)[:, None], axis=0)
    well_cells = (
        jnp.zeros((cell_count,), jnp.float32)
        .at[flat_cell]
        .add(weight.reshape(-1))
        .reshape(pressure_old.shape)
    )
    diagonal_sum = (
        storage
        + east_face
        + west_face
        + north_face
        + south_face
        + upper_face
        + lower_face
        + well_cells
    )
    base_term = storage * pressure_old - biot_coeff * strain_change
    pressure = pressure_old
    for sweep_index in range(FLOW_SWEEPS):
        padded = flow_rim(pressure)
        plane_pad = jnp.pad(pressure, ((0, 0), (1, 1), (0, 0)))
        beside = east_face * padded[2:] + west_face * padded[:-2]
        beside = beside + north_face * plane_pad[:, 2:] + south_face * plane_pad[:, :-2]
        beside = beside + upper_face * above_z(pressure) + lower_face * below_z(pressure)
        sampled = pressure.reshape(-1)[flat_cell].reshape(weight.shape)
        block_sum = jnp.sum(weight * sampled, axis=1)
        well_part = jnp.sum(member * block_sum[:, None], axis=0)
        well_sum, strength = lax.psum((well_part, strength_part), ("grp", "dev"))
        bottom = (well_rate + well_sum) / strength
        block_bottom = jnp.sum(member * bottom[None, :], axis=1)
        inflow = (
            jnp.zeros((cell_count,), jnp.float32)
            .at[flat_cell]
            .add((weight * block_bottom[:, None]).reshape(-1))
            .reshape(pressure.shape)
        )
        pressure = (base_term + beside + inflow) / diagonal_sum
    press_mech = lax.all_to_all(pressure, "dev", split_axis=1, concat_axis=0, tiled=True)
    rim_depth = 1
    wide_stack = mech_rim(jnp.stack([press_mech, modulus]), rim_depth + 1)
    force_field = forces(wide_stack[0])
    mod_wide = wide_stack[1, 1:-1, 1:-1]
    safe_modulus = jnp.where(mod_wide > 0.0, mod_wide, 1.0)
    inverse = jnp.where(mod_wide > 0.0, 1.0 / (26.0 * safe_modulus), 0.0)
    displacement = displacement_old
    for outer_round in range(MECH_SWEEPS // rim_depth):
        wide_disp = mech_rim(displacement, rim_depth)
        relaxed = trim_margin(force_field, 1) - trim_margin(mod_wide, 1) * stiffness(wide_disp)
        wide_disp = trim_margin(wide_disp, 1) + relax_factor * relaxed * trim_margin(inverse, 1)
        displacement = wide_disp
    strain_mech = divergence(mech_rim(displacement, 1))
    strain = lax.all_to_all(strain_mech, "dev", split_axis=0, concat_axis=1, tiled=True)
    return (pressure, displacement, strain)


def solution(mesh):
    return jax.shard_map(
        body,
        mesh=mesh,
        in_specs=(
            P(("grp", "dev"), None, None),
            P(("grp", "dev"), None, None),
            P(("grp", "dev"), None, None),
            P(("grp", "dev"), None, None),
            P(("grp", "dev"), None, None),
            P(("grp", "dev"), None, None),
            P(None, "grp", "dev", None),
            P("grp", "dev", None),
            P(("grp", "dev"), None),
            P(("grp", "dev")),
            P(("grp", "dev")),
            P(("grp", "dev"), None),
            P(),
        ),
        out_specs=(
            P(("grp", "dev"), None, None),
            P(None, "grp", "dev", None),
            P(("grp", "dev"), None, None),
        ),
        check_vma=False,
    )
```

profile of v0, /device:TPU:1, one launch (start us, length us, event | category | flops | bytes accessed | tf_op | source)
XLA Modules:
  0.0 580.6 jit_solution(15456460933465506291)
XLA Ops:
  0.6 4.0 collective-permute-start.2
  4.7 9.4 %collective-permute-start = (f32[1,256,256]{2,1,0:T(8,128)}, f32[1,256,256]{2,1,0:T(8,128)}, u32[]{:S(2)}, u32[]{:S(2)}) collective-permute-start(f32[1,256,256]{2,1,0:T(8,128)} %param.17), channel_id=1, source_target_pairs={{1,0},{2,1},{3,2},{4,3},{5,4},{6,5},{7,6},{8,7},{9,8},{10,9},{11,1... | collective-permute-start | bytes 786440 | tf_op jit(solution)/shard_map/ppermute | solution.py:23
  28.5 67.9 %all-reduce.54 = (f32[256]{0:T(256)S(1)}, f32[256]{0:T(256)S(1)}) all-reduce(f32[256]{0:T(256)S(1)} %get-tuple-element.33, f32[256]{0:T(256)S(1)} %get-tuple-element.32), channel_id=1, replica_groups=mesh['grp'=4,'dev'=32] {'grp','dev'}, use_global_device_ids=true, to_apply=%region_5.6 | all-reduce | flops 512 | bytes 4096 | tf_op jit(solution)/shard_map/psum | solution.py:151
  98.1 4.0 collective-permute-start.15
  102.2 3.3 scatter_custom_fusion
  105.6 3.3 scatter_custom_fusion.1
  120.3 8.6 %collective-permute-start.3 = (f32[1,256,256]{2,1,0:T(8,128)}, f32[1,256,256]{2,1,0:T(8,128)}, u32[]{:S(2)}, u32[]{:S(2)}) collective-permute-start(f32[1,256,256]{2,1,0:T(8,128)} %get-tuple-element.62), channel_id=1, source_target_pairs={{1,0},{2,1},{3,2},{4,3},{5,4},{6,5},{7,6},{8,7},{9,8},{10,9},{11,1... | collective-permute-start | bytes 786440 | tf_op jit(solution)/shard_map/ppermute | solution.py:23
  132.5 66.3 %psum.36 = f32[256]{0:T(256)S(1)} all-reduce(f32[256]{0:T(256)S(1)} %select_reduce_fusion.5), channel_id=1, replica_groups=mesh['grp'=4,'dev'=32] {'grp','dev'}, use_global_device_ids=true, to_apply=%region_11.12 | all-reduce | flops 256 | bytes 2048 | tf_op jit(solution)/shard_map/psum | solution.py:151
  199.1 3.8 scatter_custom_fusion.2
  209.5 8.3 %collective-permute-start.5 = (f32[1,256,256]{2,1,0:T(8,128)S(1)}, f32[1,256,256]{2,1,0:T(8,128)}, u32[]{:S(2)}, u32[]{:S(2)}) collective-permute-start(f32[1,256,256]{2,1,0:T(8,128)S(1)} %add_divide_fusion.2), channel_id=1, source_target_pairs={{1,0},{2,1},{3,2},{4,3},{5,4},{6,5},{7,6},{8,7},{9,8},{10,9},{11,1... | collective-permute-start | bytes 786440 | tf_op jit(solution)/shard_map/ppermute | solution.py:23
  221.4 64.2 %psum.39 = f32[256]{0:T(256)S(1)} all-reduce(f32[256]{0:T(256)S(1)} %select_reduce_fusion.3), channel_id=1, replica_groups=mesh['grp'=4,'dev'=32] {'grp','dev'}, use_global_device_ids=true, to_apply=%region_16.17 | all-reduce | flops 256 | bytes 2048 | tf_op jit(solution)/shard_map/psum | solution.py:151
  285.8 3.9 scatter_custom_fusion.3
  295.3 9.4 %collective-permute-start.7 = (f32[1,256,256]{2,1,0:T(8,128)S(1)}, f32[1,256,256]{2,1,0:T(8,128)}, u32[]{:S(2)}, u32[]{:S(2)}) collective-permute-start(f32[1,256,256]{2,1,0:T(8,128)S(1)} %add_divide_fusion.1), channel_id=1, source_target_pairs={{1,0},{2,1},{3,2},{4,3},{5,4},{6,5},{7,6},{8,7},{9,8},{10,9},{11,1... | collective-permute-start | bytes 786440 | tf_op jit(solution)/shard_map/ppermute | solution.py:23
  308.2 62.3 %psum.48 = f32[256]{0:T(256)S(1)} all-reduce(f32[256]{0:T(256)S(1)} %select_reduce_fusion.1), channel_id=1, replica_groups=mesh['grp'=4,'dev'=32] {'grp','dev'}, use_global_device_ids=true, to_apply=%region_21.22 | all-reduce | flops 256 | bytes 2048 | tf_op jit(solution)/shard_map/psum | solution.py:151
  370.8 3.9 scatter_custom_fusion.4
  379.9 5.0 all-to-all-start
  386.4 7.9 %all-to-all-done = f32[1,256,256]{2,0,1:T(1,128)S(1)} async-done(((f32[1,256,256]{2,0,1:T(1,128)}), f32[1,256,256]{2,0,1:T(1,128)S(1)}, u32[]{:S(2)}, u32[]{:S(2)}) %all-to-all-start) | async-done | bytes 262176 | tf_op jit(solution)/shard_map/all_to_all | solution.py:161
  394.4 4.0 collective-permute-start.10
  402.9 4.0 collective-permute-start.11
  415.0 3.4 collective-permute-start.17
  420.8 4.9 collective-permute-start.19
  432.8 4.6 collective-permute-start.21
  439.8 4.7 collective-permute-start.23
  451.3 5.1 collective-permute-start.25
  458.8 4.7 collective-permute-start.27
  470.3 5.1 collective-permute-start.29
  477.7 4.9 collective-permute-start.31
  489.3 5.1 collective-permute-start.33
  496.7 6.5 %collective-permute-start.35 = (f32[3,34,1,256]{3,2,1,0:T(1,128)S(1)}, f32[3,34,1,256]{3,2,1,0:T(1,128)S(1)}, u32[]{:S(2)}, u32[]{:S(2)}) collective-permute-start(f32[3,34,1,256]{3,2,1,0:T(1,128)S(1)} %get-tuple-element.81), channel_id=1, source_target_pairs={{0,1},{1,2},{2,3},{3,4},{4,5},{5,6},{6,7},{7,8},{8,9},{9,10},{10,1... | collective-permute-start | bytes 313352 | tf_op jit(solution)/shard_map/ppermute | solution.py:20
  510.0 5.1 collective-permute-start.37
  517.4 6.8 %collective-permute-start.39 = (f32[3,34,1,256]{3,2,1,0:T(1,128)S(1)}, f32[3,34,1,256]{3,2,1,0:T(1,128)S(1)}, u32[]{:S(2)}, u32[]{:S(2)}) collective-permute-start(f32[3,34,1,256]{3,2,1,0:T(1,128)S(1)} %get-tuple-element.79), channel_id=1, source_target_pairs={{0,1},{1,2},{2,3},{3,4},{4,5},{5,6},{6,7},{7,8},{8,9},{9,10},{10,1... | collective-permute-start | bytes 313352 | tf_op jit(solution)/shard_map/ppermute | solution.py:20
  526.6 53.0 %all_to_all.24 = f32[32,8,256]{2,1,0:T(8,128)S(1)} all-to-all(f32[32,8,256]{2,1,0:T(8,128)S(1)} %fusion.75), channel_id=1, replica_groups=mesh['grp'=4,'dev'=32] {'dev'}, dimensions={0} | all-to-all | bytes 524288 | tf_op jit(solution)/shard_map/all_to_all | solution.py:175
  (298 shorter events, 120.5 us)
Async XLA Ops:
  0.6 113.3 %collective-permute-start.2 = (f32[1,256,256]{2,1,0:T(8,128)}, f32[1,256,256]{2,1,0:T(8,128)S(1)}, u32[]{:S(2)}, u32[]{:S(2)}) collective-permute-start(f32[1,256,256]{2,1,0:T(8,128)} %param.17), channel_id=1, source_target_pairs={{0,1},{1,2},{2,3},{3,4},{4,5},{5,6},{6,7},{7,8},{8,9},{9,10},{10,1... | collective-permute-start | bytes 786440 | tf_op jit(solution)/shard_map/ppermute | solution.py:20
  4.7 109.3 %collective-permute-start = (f32[1,256,256]{2,1,0:T(8,128)}, f32[1,256,256]{2,1,0:T(8,128)}, u32[]{:S(2)}, u32[]{:S(2)}) collective-permute-start(f32[1,256,256]{2,1,0:T(8,128)} %param.17), channel_id=1, source_target_pairs={{1,0},{2,1},{3,2},{4,3},{5,4},{6,5},{7,6},{8,7},{9,8},{10,9},{11,1... | collective-permute-start | bytes 786440 | tf_op jit(solution)/shard_map/ppermute | solution.py:23
  14.1 99.8 %collective-permute-start.1 = (f32[1,256,256]{2,1,0:T(8,128)}, f32[1,256,256]{2,1,0:T(8,128)S(1)}, u32[]{:S(2)}, u32[]{:S(2)}) collective-permute-start(f32[1,256,256]{2,1,0:T(8,128)} %param.20), channel_id=1, source_target_pairs={{0,1},{1,2},{2,3},{3,4},{4,5},{5,6},{6,7},{7,8},{8,9},{9,10},{10,1... | collective-permute-start | bytes 786440 | tf_op jit(solution)/shard_map/ppermute | solution.py:20
  16.8 79.7 %collective-permute-start.13 = (f32[3,1,8,256]{3,2,1,0:T(8,128)S(1)}, f32[3,1,8,256]{3,2,1,0:T(8,128)S(1)}, u32[]{:S(2)}, u32[]{:S(2)}) collective-permute-start(f32[3,1,8,256]{3,2,1,0:T(8,128)S(1)} %get-tuple-element.106), channel_id=1, source_target_pairs={{0,32},{32,64},{64,96},{1,33},{33,65},{65,97},{2,34},{34,66},{66,9... | collective-permute-start | bytes 73736 | tf_op jit(solution)/shard_map/ppermute | solution.py:20
  18.8 77.9 %collective-permute-start.14 = (f32[3,1,8,256]{3,2,1,0:T(8,128)S(1)}, f32[3,1,8,256]{3,2,1,0:T(8,128)S(1)}, u32[]{:S(2)}, u32[]{:S(2)}) collective-permute-start(f32[3,1,8,256]{3,2,1,0:T(8,128)S(1)} %get-tuple-element.105), channel_id=1, source_target_pairs={{32,0},{64,32},{96,64},{33,1},{65,33},{97,65},{34,2},{66,34},{98,6... | collective-permute-start | bytes 73736 | tf_op jit(solution)/shard_map/ppermute | solution.py:23
  96.8 13.7 %collective-permute-start.16 = (f32[3,34,1,256]{3,2,1,0:T(1,128)S(1)}, f32[3,34,1,256]{3,2,1,0:T(1,128)S(1)}, u32[]{:S(2)}, u32[]{:S(2)}) collective-permute-start(f32[3,34,1,256]{3,2,1,0:T(1,128)S(1)} %get-tuple-element.92), channel_id=1, source_target_pairs={{1,0},{2,1},{3,2},{4,3},{5,4},{6,5},{7,6},{8,7},{9,8},{10,9},{11,1... | collective-permute-start | bytes 313352 | tf_op jit(solution)/shard_map/ppermute | solution.py:23
  98.1 12.4 %collective-permute-start.15 = (f32[3,34,1,256]{3,2,1,0:T(1,128)S(1)}, f32[3,34,1,256]{3,2,1,0:T(1,128)S(1)}, u32[]{:S(2)}, u32[]{:S(2)}) collective-permute-start(f32[3,34,1,256]{3,2,1,0:T(1,128)S(1)} %get-tuple-element.91), channel_id=1, source_target_pairs={{0,1},{1,2},{2,3},{3,4},{4,5},{5,6},{6,7},{7,8},{8,9},{9,10},{10,1... | collective-permute-start | bytes 313352 | tf_op jit(solution)/shard_map/ppermute | solution.py:20
  117.6 87.2 %collective-permute-start.4 = (f32[1,256,256]{2,1,0:T(8,128)}, f32[1,256,256]{2,1,0:T(8,128)}, u32[]{:S(2)}, u32[]{:S(2)}) collective-permute-start(f32[1,256,256]{2,1,0:T(8,128)} %get-tuple-element.62), channel_id=1, source_target_pairs={{0,1},{1,2},{2,3},{3,4},{4,5},{5,6},{6,7},{7,8},{8,9},{9,10},{10,1... | collective-permute-start | bytes 786440 | tf_op jit(solution)/shard_map/ppermute | solution.py:20
  120.3 84.6 %collective-permute-start.3 = (f32[1,256,256]{2,1,0:T(8,128)}, f32[1,256,256]{2,1,0:T(8,128)}, u32[]{:S(2)}, u32[]{:S(2)}) collective-permute-start(f32[1,256,256]{2,1,0:T(8,128)} %get-tuple-element.62), channel_id=1, source_target_pairs={{1,0},{2,1},{3,2},{4,3},{5,4},{6,5},{7,6},{8,7},{9,8},{10,9},{11,1... | collective-permute-start | bytes 786440 | tf_op jit(solution)/shard_map/ppermute | solution.py:23
  206.6 85.1 %collective-permute-start.6 = (f32[1,256,256]{2,1,0:T(8,128)S(1)}, f32[1,256,256]{2,1,0:T(8,128)}, u32[]{:S(2)}, u32[]{:S(2)}) collective-permute-start(f32[1,256,256]{2,1,0:T(8,128)S(1)} %add_divide_fusion.2), channel_id=1, source_target_pairs={{0,1},{1,2},{2,3},{3,4},{4,5},{5,6},{6,7},{7,8},{8,9},{9,10},{10,1... | collective-permute-start | bytes 786440 | tf_op jit(solution)/shard_map/ppermute | solution.py:20
  209.5 82.1 %collective-permute-start.5 = (f32[1,256,256]{2,1,0:T(8,128)S(1)}, f32[1,256,256]{2,1,0:T(8,128)}, u32[]{:S(2)}, u32[]{:S(2)}) collective-permute-start(f32[1,256,256]{2,1,0:T(8,128)S(1)} %add_divide_fusion.2), channel_id=1, source_target_pairs={{1,0},{2,1},{3,2},{4,3},{5,4},{6,5},{7,6},{8,7},{9,8},{10,9},{11,1... | collective-permute-start | bytes 786440 | tf_op jit(solution)/shard_map/ppermute | solution.py:23
  293.4 83.2 %collective-permute-start.8 = (f32[1,256,256]{2,1,0:T(8,128)S(1)}, f32[1,256,256]{2,1,0:T(8,128)}, u32[]{:S(2)}, u32[]{:S(2)}) collective-permute-start(f32[1,256,256]{2,1,0:T(8,128)S(1)} %add_divide_fusion.1), channel_id=1, source_target_pairs={{0,1},{1,2},{2,3},{3,4},{4,5},{5,6},{6,7},{7,8},{8,9},{9,10},{10,1... | collective-permute-start | bytes 786440 | tf_op jit(solution)/shard_map/ppermute | solution.py:20
  295.3 81.3 %collective-permute-start.7 = (f32[1,256,256]{2,1,0:T(8,128)S(1)}, f32[1,256,256]{2,1,0:T(8,128)}, u32[]{:S(2)}, u32[]{:S(2)}) collective-permute-start(f32[1,256,256]{2,1,0:T(8,128)S(1)} %add_divide_fusion.1), channel_id=1, source_target_pairs={{1,0},{2,1},{3,2},{4,3},{5,4},{6,5},{7,6},{8,7},{9,8},{10,9},{11,1... | collective-permute-start | bytes 786440 | tf_op jit(solution)/shard_map/ppermute | solution.py:23
  379.9 14.5 %all-to-all-start = ((f32[1,256,256]{2,0,1:T(1,128)}), f32[1,256,256]{2,0,1:T(1,128)S(1)}, u32[]{:S(2)}, u32[]{:S(2)}) async-start(f32[1,256,256]{2,0,1:T(1,128)} %copy.36), calls=%async_computation | async-start | bytes 524288 | tf_op jit(solution)/shard_map/all_to_all | solution.py:161
  401.6 7.2 %collective-permute-start.12 = (f32[2,36,2,256]{3,2,1,0:T(2,128)S(1)}, f32[2,36,2,256]{3,2,1,0:T(2,128)S(1)}, u32[]{:S(2)}, u32[]{:S(2)}) collective-permute-start(f32[2,36,2,256]{3,2,1,0:T(2,128)S(1)} %get-tuple-element.112), channel_id=1, source_target_pairs={{1,0},{2,1},{3,2},{4,3},{5,4},{6,5},{7,6},{8,7},{9,8},{10,9},{11,1... | collective-permute-start | bytes 442376 | tf_op jit(solution)/shard_map/ppermute | solution.py:23
  402.9 6.8 %collective-permute-start.11 = (f32[2,36,2,256]{3,2,1,0:T(2,128)S(1)}, f32[2,36,2,256]{3,2,1,0:T(2,128)S(1)}, u32[]{:S(2)}, u32[]{:S(2)}) collective-permute-start(f32[2,36,2,256]{3,2,1,0:T(2,128)S(1)} %get-tuple-element.111), channel_id=1, source_target_pairs={{0,1},{1,2},{2,3},{3,4},{4,5},{5,6},{6,7},{7,8},{8,9},{9,10},{10,1... | collective-permute-start | bytes 442376 | tf_op jit(solution)/shard_map/ppermute | solution.py:20
  411.8 6.6 %collective-permute-start.18 = (f32[3,1,8,256]{3,2,1,0:T(8,128)S(1)}, f32[3,1,8,256]{3,2,1,0:T(8,128)S(1)}, u32[]{:S(2)}, u32[]{:S(2)}) collective-permute-start(f32[3,1,8,256]{3,2,1,0:T(8,128)S(1)} %get-tuple-element.104), channel_id=1, source_target_pairs={{32,0},{64,32},{96,64},{33,1},{65,33},{97,65},{34,2},{66,34},{98,6... | collective-permute-start | bytes 73736 | tf_op jit(solution)/shard_map/ppermute | solution.py:23
  419.5 6.4 %collective-permute-start.20 = (f32[3,34,1,256]{3,2,1,0:T(1,128)S(1)}, f32[3,34,1,256]{3,2,1,0:T(1,128)S(1)}, u32[]{:S(2)}, u32[]{:S(2)}) collective-permute-start(f32[3,34,1,256]{3,2,1,0:T(1,128)S(1)} %get-tuple-element.90), channel_id=1, source_target_pairs={{1,0},{2,1},{3,2},{4,3},{5,4},{6,5},{7,6},{8,7},{9,8},{10,9},{11,1... | collective-permute-start | bytes 313352 | tf_op jit(solution)/shard_map/ppermute | solution.py:23
  420.8 6.8 %collective-permute-start.19 = (f32[3,34,1,256]{3,2,1,0:T(1,128)S(1)}, f32[3,34,1,256]{3,2,1,0:T(1,128)S(1)}, u32[]{:S(2)}, u32[]{:S(2)}) collective-permute-start(f32[3,34,1,256]{3,2,1,0:T(1,128)S(1)} %get-tuple-element.89), channel_id=1, source_target_pairs={{0,1},{1,2},{2,3},{3,4},{4,5},{5,6},{6,7},{7,8},{8,9},{9,10},{10,1... | collective-permute-start | bytes 313352 | tf_op jit(solution)/shard_map/ppermute | solution.py:20
  430.9 6.6 %collective-permute-start.22 = (f32[3,1,8,256]{3,2,1,0:T(8,128)S(1)}, f32[3,1,8,256]{3,2,1,0:T(8,128)S(1)}, u32[]{:S(2)}, u32[]{:S(2)}) collective-permute-start(f32[3,1,8,256]{3,2,1,0:T(8,128)S(1)} %get-tuple-element.102), channel_id=1, source_target_pairs={{32,0},{64,32},{96,64},{33,1},{65,33},{97,65},{34,2},{66,34},{98,6... | collective-permute-start | bytes 73736 | tf_op jit(solution)/shard_map/ppermute | solution.py:23
  439.8 6.4 %collective-permute-start.23 = (f32[3,34,1,256]{3,2,1,0:T(1,128)S(1)}, f32[3,34,1,256]{3,2,1,0:T(1,128)S(1)}, u32[]{:S(2)}, u32[]{:S(2)}) collective-permute-start(f32[3,34,1,256]{3,2,1,0:T(1,128)S(1)} %get-tuple-element.87), channel_id=1, source_target_pairs={{0,1},{1,2},{2,3},{3,4},{4,5},{5,6},{6,7},{7,8},{8,9},{9,10},{10,1... | collective-permute-start | bytes 313352 | tf_op jit(solution)/shard_map/ppermute | solution.py:20
  449.4 7.0 %collective-permute-start.26 = (f32[3,1,8,256]{3,2,1,0:T(8,128)S(1)}, f32[3,1,8,256]{3,2,1,0:T(8,128)S(1)}, u32[]{:S(2)}, u32[]{:S(2)}) collective-permute-start(f32[3,1,8,256]{3,2,1,0:T(8,128)S(1)} %get-tuple-element.100), channel_id=1, source_target_pairs={{32,0},{64,32},{96,64},{33,1},{65,33},{97,65},{34,2},{66,34},{98,6... | collective-permute-start | bytes 73736 | tf_op jit(solution)/shard_map/ppermute | solution.py:23
  458.8 6.4 %collective-permute-start.27 = (f32[3,34,1,256]{3,2,1,0:T(1,128)S(1)}, f32[3,34,1,256]{3,2,1,0:T(1,128)S(1)}, u32[]{:S(2)}, u32[]{:S(2)}) collective-permute-start(f32[3,34,1,256]{3,2,1,0:T(1,128)S(1)} %get-tuple-element.85), channel_id=1, source_target_pairs={{0,1},{1,2},{2,3},{3,4},{4,5},{5,6},{6,7},{7,8},{8,9},{9,10},{10,1... | collective-permute-start | bytes 313352 | tf_op jit(solution)/shard_map/ppermute | solution.py:20
  468.4 7.0 %collective-permute-start.30 = (f32[3,1,8,256]{3,2,1,0:T(8,128)S(1)}, f32[3,1,8,256]{3,2,1,0:T(8,128)S(1)}, u32[]{:S(2)}, u32[]{:S(2)}) collective-permute-start(f32[3,1,8,256]{3,2,1,0:T(8,128)S(1)} %get-tuple-element.98), channel_id=1, source_target_pairs={{32,0},{64,32},{96,64},{33,1},{65,33},{97,65},{34,2},{66,34},{98,6... | collective-permute-start | bytes 73736 | tf_op jit(solution)/shard_map/ppermute | solution.py:23
  476.4 6.2 %collective-permute-start.32 = (f32[3,34,1,256]{3,2,1,0:T(1,128)S(1)}, f32[3,34,1,256]{3,2,1,0:T(1,128)S(1)}, u32[]{:S(2)}, u32[]{:S(2)}) collective-permute-start(f32[3,34,1,256]{3,2,1,0:T(1,128)S(1)} %get-tuple-element.84), channel_id=1, source_target_pairs={{1,0},{2,1},{3,2},{4,3},{5,4},{6,5},{7,6},{8,7},{9,8},{10,9},{11,1... | collective-permute-start | bytes 313352 | tf_op jit(solution)/shard_map/ppermute | solution.py:23
  477.7 6.4 %collective-permute-start.31 = (f32[3,34,1,256]{3,2,1,0:T(1,128)S(1)}, f32[3,34,1,256]{3,2,1,0:T(1,128)S(1)}, u32[]{:S(2)}, u32[]{:S(2)}) collective-permute-start(f32[3,34,1,256]{3,2,1,0:T(1,128)S(1)} %get-tuple-element.83), channel_id=1, source_target_pairs={{0,1},{1,2},{2,3},{3,4},{4,5},{5,6},{6,7},{7,8},{8,9},{9,10},{10,1... | collective-permute-start | bytes 313352 | tf_op jit(solution)/shard_map/ppermute | solution.py:20
  487.3 7.0 %collective-permute-start.34 = (f32[3,1,8,256]{3,2,1,0:T(8,128)S(1)}, f32[3,1,8,256]{3,2,1,0:T(8,128)S(1)}, u32[]{:S(2)}, u32[]{:S(2)}) collective-permute-start(f32[3,1,8,256]{3,2,1,0:T(8,128)S(1)} %get-tuple-element.96), channel_id=1, source_target_pairs={{32,0},{64,32},{96,64},{33,1},{65,33},{97,65},{34,2},{66,34},{98,6... | collective-permute-start | bytes 73736 | tf_op jit(solution)/shard_map/ppermute | solution.py:23
  495.4 7.9 %collective-permute-start.36 = (f32[3,34,1,256]{3,2,1,0:T(1,128)S(1)}, f32[3,34,1,256]{3,2,1,0:T(1,128)S(1)}, u32[]{:S(2)}, u32[]{:S(2)}) collective-permute-start(f32[3,34,1,256]{3,2,1,0:T(1,128)S(1)} %get-tuple-element.82), channel_id=1, source_target_pairs={{1,0},{2,1},{3,2},{4,3},{5,4},{6,5},{7,6},{8,7},{9,8},{10,9},{11,1... | collective-permute-start | bytes 313352 | tf_op jit(solution)/shard_map/ppermute | solution.py:23
  496.7 8.1 %collective-permute-start.35 = (f32[3,34,1,256]{3,2,1,0:T(1,128)S(1)}, f32[3,34,1,256]{3,2,1,0:T(1,128)S(1)}, u32[]{:S(2)}, u32[]{:S(2)}) collective-permute-start(f32[3,34,1,256]{3,2,1,0:T(1,128)S(1)} %get-tuple-element.81), channel_id=1, source_target_pairs={{0,1},{1,2},{2,3},{3,4},{4,5},{5,6},{6,7},{7,8},{8,9},{9,10},{10,1... | collective-permute-start | bytes 313352 | tf_op jit(solution)/shard_map/ppermute | solution.py:20
  508.1 7.3 %collective-permute-start.38 = (f32[3,1,8,256]{3,2,1,0:T(8,128)S(1)}, f32[3,1,8,256]{3,2,1,0:T(8,128)S(1)}, u32[]{:S(2)}, u32[]{:S(2)}) collective-permute-start(f32[3,1,8,256]{3,2,1,0:T(8,128)S(1)} %get-tuple-element.94), channel_id=1, source_target_pairs={{32,0},{64,32},{96,64},{33,1},{65,33},{97,65},{34,2},{66,34},{98,6... | collective-permute-start | bytes 73736 | tf_op jit(solution)/shard_map/ppermute | solution.py:23
  516.1 8.2 %collective-permute-start.40 = (f32[3,34,1,256]{3,2,1,0:T(1,128)S(1)}, f32[3,34,1,256]{3,2,1,0:T(1,128)S(1)}, u32[]{:S(2)}, u32[]{:S(2)}) collective-permute-start(f32[3,34,1,256]{3,2,1,0:T(1,128)S(1)} %get-tuple-element.80), channel_id=1, source_target_pairs={{1,0},{2,1},{3,2},{4,3},{5,4},{6,5},{7,6},{8,7},{9,8},{10,9},{11,1... | collective-permute-start | bytes 313352 | tf_op jit(solution)/shard_map/ppermute | solution.py:23
  517.4 8.5 %collective-permute-start.39 = (f32[3,34,1,256]{3,2,1,0:T(1,128)S(1)}, f32[3,34,1,256]{3,2,1,0:T(1,128)S(1)}, u32[]{:S(2)}, u32[]{:S(2)}) collective-permute-start(f32[3,34,1,256]{3,2,1,0:T(1,128)S(1)} %get-tuple-element.79), channel_id=1, source_target_pairs={{0,1},{1,2},{2,3},{3,4},{4,5},{5,6},{6,7},{7,8},{8,9},{9,10},{10,1... | collective-permute-start | bytes 313352 | tf_op jit(solution)/shard_map/ppermute | solution.py:20
  (46 other events, 646.8 us)
where the time goes:
time: 592 us; the launch traced here: 581 us
  blocking collectives  314 us (53%)
  starting transfers between devices  157 us (27%)
  other arithmetic  45.5 us (8%)
  local copies, waits for them, and re-layouts  35.2 us (6%)
  waiting for transfers between devices  27 us (5%)
    psum x4, blocking collectives, body(): well_sum, strength = lax.psum((well_part, strength_part), ('grp', 'dev'))  261 us
    ppermute x21, starting transfers between devices, padded_2(): lax.ppermute(lax.slice_in_dim(block, block.shape[dim] - width, None, axis...  86.1 us
    ppermute x20, starting transfers between devices, padded_2(): lax.ppermute(lax.slice_in_dim(block, 0, width, axis=dim), axis, backward)  65.4 us
    all_to_all x1, blocking collectives, body(): lax.all_to_all(strain_mech, 'dev', split_axis=0, concat_axis=1, tiled=True)  53 us
    ppermute x21, waiting for transfers between devices, padded_2(): lax.ppermute(lax.slice_in_dim(block, block.shape[dim] - width, None, axis...  16.4 us
    scatter-add x4, other arithmetic, body(): inflow = jnp.zeros((cell_count,), jnp.float32).at[flat_cell].add((weight...  15 us
    gather x4, local copies, waits for them, and re-layouts, body(): sampled = pressure.reshape(-1)[flat_cell].reshape(weight.shape)  12.6 us
  transfers between devices with their start and end apart: 42, of which 22 were waited for; matrix products, arithmetic and copies ran while one was open for 9% of the time, Pallas kernels for 0%

commit v1 on v0

v1 whole, which is shorter than its diff:
```python
import functools

import jax
import jax.numpy as jnp
from jax import lax
from jax.experimental import pallas as pl
from jax.experimental.pallas import tpu as pltpu
from jax.sharding import PartitionSpec as P

MESH = pl.DeviceIdType.MESH
F32 = jnp.float32

FLOW_SWEEPS = 4
MECH_SWEEPS = 6
BIOT = 0.8
RELAX = 0.6
COUPLE = 0.375

NG, ND = 4, 32
NF = NG * ND
NY, NZ = 256, 256
XS, YS = 32, 8
HALO = MECH_SWEEPS + 1
XW = XS + 2 * HALO
YW = 3 * YS
BLOCKS = 4

ALPHA = 1.0 - RELAX * 27.0 / 26.0
BETA = RELAX / 26.0


def iota(shape, dim):
    return lax.broadcasted_iota(jnp.int32, shape, dim)


def next_z(v):
    n = v.shape[-1]
    return jnp.where(iota(v.shape, 1) == n - 1, 0.0, pltpu.roll(v, n - 1, 1))


def prev_z(v):
    return jnp.where(iota(v.shape, 1) == 0, 0.0, pltpu.roll(v, 1, 1))


def next_y(v):
    return pltpu.roll(v, v.shape[0] - 1, 0)


def prev_y(v):
    return pltpu.roll(v, 1, 0)


def total(v):
    return jnp.sum(jnp.sum(v, axis=0, keepdims=True), axis=1, keepdims=True)


def kernel(
    p0_h, sc_h, st_h, tx_h, ty_h, tz_h, u_h, mod_h, cell_ref, well_ref, cnt_ref, idx_ref, rate_ref,
    p_out, u_out, s_out,
    press, base, east, west, north, south, upper, lower, rdiag, wells, halo_lo, halo_hi,
    msg0, msg, ag0, ag, masks,
    ppad, pwin, ua, ub, mod, gain, force, tzb, dzb, strain,
    load_sem, uload_sem, halo_send, halo_recv, tx_send, tx_recv, ag_send, ag_recv,
    usend, urecv, xsend, xrecv, pw_send, pw_recv, pw_self, st_send, st_recv, st_self, out_sem,
):
    g = lax.axis_index("grp")
    d = lax.axis_index("dev")
    f = g * ND + d
    first, last = f == 0, f == NF - 1

    def flow_dev(k):
        return (k // ND, lax.rem(k, ND))

    after, before = flow_dev(lax.rem(f + 1, NF)), flow_dev(lax.rem(f + NF - 1, NF))

    plane_loads = [
        pltpu.make_async_copy(src.at[0], dst, load_sem.at[i])
        for i, (src, dst) in enumerate(
            [
                (p0_h, press.at[0]),
                (sc_h, base),
                (st_h, rdiag),
                (tx_h, east),
                (ty_h, north),
                (tz_h, upper),
            ]
        )
    ]
    for c in plane_loads:
        c.start()
    own_u = pltpu.make_async_copy(
        u_h, ua.at[:, pl.ds(HALO, XS), pl.ds(YS, YS)], uload_sem.at[0]
    )
    own_m = pltpu.make_async_copy(
        mod_h, mod.at[pl.ds(HALO, XS), pl.ds(YS, YS)], uload_sem.at[1]
    )
    own_u.start()
    own_m.start()

    barrier = pltpu.get_barrier_semaphore()

    def greet(i, carry):
        pl.semaphore_signal(
            barrier, inc=1, device_id=flow_dev(lax.rem(f + i, NF)), device_id_type=MESH
        )
        return carry

    lax.fori_loop(1, NF, greet, 0)

    @pl.when(d == 0)
    def _():
        ua[:, HALO : HALO + XS, 0:YS, :] = jnp.zeros((3, XS, YS, NZ), F32)
        mod[HALO : HALO + XS, 0:YS, :] = jnp.ones((XS, YS, NZ), F32)

    @pl.when(d == ND - 1)
    def _():
        ua[:, HALO : HALO + XS, 2 * YS :, :] = jnp.zeros((3, XS, YS, NZ), F32)
        mod[HALO : HALO + XS, 2 * YS :, :] = jnp.ones((XS, YS, NZ), F32)

    @pl.when(g == 0)
    def _():
        ua[:, 0:HALO] = jnp.zeros((3, HALO, YW, NZ), F32)
        mod[0:HALO] = jnp.ones((HALO, YW, NZ), F32)
        pwin[0:HALO] = jnp.zeros((HALO, YW, NZ), F32)

    @pl.when(g == NG - 1)
    def _():
        ua[:, HALO + XS :] = jnp.zeros((3, HALO, YW, NZ), F32)
        mod[HALO + XS :] = jnp.ones((HALO, YW, NZ), F32)
        pwin[HALO + XS :] = jnp.zeros((HALO, YW, NZ), F32)

    @pl.when(first)
    def _():
        halo_lo[...] = jnp.zeros(halo_lo.shape, F32)
        west[...] = jnp.zeros((NY, NZ), F32)

    @pl.when(last)
    def _():
        halo_hi[...] = jnp.zeros(halo_hi.shape, F32)

    ppad[0:YS, :] = jnp.zeros((YS, NZ), F32)
    ppad[NY + YS :, :] = jnp.zeros((YS, NZ), F32)

    lane = iota((1, 128), 1)
    weight_sums = []
    for b in range(BLOCKS):
        live = lane < cnt_ref[b : b + 1, :]
        weight = jnp.where(live, idx_ref[b : b + 1, :], 0.0)
        cell = cell_ref[b : b + 1, :]
        row, col = cell // NZ, lax.rem(cell, NZ)
        at_row = iota((NY, 128), 0) == row
        at_col = jnp.where(iota((NZ, 128), 0) == col, 1.0, 0.0).astype(jnp.bfloat16)
        rest = weight
        plane = jnp.zeros((NY, NZ), F32)
        for _ in range(3):
            part = rest.astype(jnp.bfloat16)
            rest = rest - part.astype(F32)
            spread = jnp.where(at_row, part.astype(F32), 0.0).astype(jnp.bfloat16)
            plane = plane + lax.dot_general(
                spread, at_col, (((1,), (1,)), ((), ())), preferred_element_type=F32
            )
        wells[b] = plane
        weight_sums.append(jnp.sum(weight, axis=1, keepdims=True))

    pl.semaphore_wait(barrier, NF - 1)

    for c in plane_loads:
        c.wait()

    def halo_copies(k):
        up = pltpu.make_async_remote_copy(
            press.at[k], halo_lo.at[k], halo_send.at[0, k], halo_recv.at[0, k],
            device_id=after, device_id_type=MESH,
        )
        down = pltpu.make_async_remote_copy(
            press.at[k], halo_hi.at[k], halo_send.at[1, k], halo_recv.at[1, k],
            device_id=before, device_id_type=MESH,
        )
        return up, down

    tx_copy = pltpu.make_async_remote_copy(
        tx_h.at[0], west, tx_send, tx_recv, device_id=after, device_id_type=MESH
    )

    def start_halo(k):
        up, down = halo_copies(k)

        @pl.when(jnp.logical_not(last))
        def _():
            up.start()

        @pl.when(jnp.logical_not(first))
        def _():
            down.start()

    def wait_halo(k):
        up, down = halo_copies(k)

        @pl.when(jnp.logical_not(first))
        def _():
            up.wait_recv()

        @pl.when(jnp.logical_not(last))
        def _():
            down.wait_recv()

    def wait_halo_send(k):
        up, down = halo_copies(k)

        @pl.when(jnp.logical_not(last))
        def _():
            up.wait_send()

        @pl.when(jnp.logical_not(first))
        def _():
            down.wait_send()

    def lanes(values):
        out = jnp.zeros((1, 128), F32)
        for j, v in enumerate(values):
            out = jnp.where(lane == j, v, out)
        return out

    def block_sums(k):
        p = press[k]
        return [total(wells[b] * p) for b in range(BLOCKS)]

    def start_gather(k):
        src = msg0 if k == 0 else msg.at[k - 1]
        dst = ag0 if k == 0 else ag.at[k - 1]

        def send(i, carry):
            pltpu.make_async_remote_copy(
                src, dst.at[f], ag_send.at[k], ag_recv.at[k],
                device_id=flow_dev(lax.rem(f + i, NF)), device_id_type=MESH,
            ).start()
            return carry

        lax.fori_loop(1, NF, send, 0)

    def gather_wait(k, sem):
        dst = ag0 if k == 0 else ag.at[k - 1]
        part = dst.at[pl.ds(0, NF - 1)]
        pltpu.make_async_copy(part, part, sem).wait()

    @pl.when(jnp.logical_not(last))
    def _():
        tx_copy.start()

    start_halo(0)
    well_ids = [well_ref[b : b + 1, :].astype(F32) for b in range(BLOCKS)]
    msg0[:, 0:128] = lanes(block_sums(0))
    msg0[:, 128:256] = lanes(weight_sums)
    msg0[:, 256:384] = jnp.where(lane < BLOCKS, lanes(well_ids), -1.0)
    ag0[f] = msg0[...]
    start_gather(0)

    has_lo, has_hi = d > 0, d < ND - 1

    def y_copies(up):
        target = (g, lax.rem(d + 1, ND)) if up else (g, lax.rem(d + ND - 1, ND))
        at = 0 if up else 2 * YS
        s = 0 if up else 1
        return (
            pltpu.make_async_remote_copy(
                u_h, ua.at[:, pl.ds(HALO, XS), pl.ds(at, YS)], usend.at[s, 0], urecv.at[s, 0],
                device_id=target, device_id_type=MESH,
            ),
            pltpu.make_async_remote_copy(
                mod_h, mod.at[pl.ds(HALO, XS), pl.ds(at, YS)], usend.at[s, 1], urecv.at[s, 1],
                device_id=target, device_id_type=MESH,
            ),
        )

    def x_copies(up):
        target = (lax.rem(g + 1, NG), d) if up else (lax.rem(g + NG - 1, NG), d)
        src = XS if up else HALO
        dst = 0 if up else HALO + XS
        s = 0 if up else 1
        return (
            pltpu.make_async_remote_copy(
                ua.at[:, pl.ds(src, HALO)], ua.at[:, pl.ds(dst, HALO)], xsend.at[s, 0], xrecv.at[s, 0],
                device_id=target, device_id_type=MESH,
            ),
            pltpu.make_async_remote_copy(
                mod.at[pl.ds(src, HALO)], mod.at[pl.ds(dst, HALO)], xsend.at[s, 1], xrecv.at[s, 1],
                device_id=target, device_id_type=MESH,
            ),
        )

    @pl.when(has_hi)
    def _():
        for c in y_copies(True):
            c.start()

    @pl.when(has_lo)
    def _():
        for c in y_copies(False):
            c.start()

    p0 = press[0]
    storage = rdiag[...]
    base[...] = storage * p0 - BIOT * base[...]
    east[...] = jnp.where(last, 0.0, east[...])
    north[...] = jnp.where(iota((NY, NZ), 0) == NY - 1, 0.0, north[...])
    south[...] = prev_y(north[...])
    upper[...] = jnp.where(iota((NY, NZ), 1) == NZ - 1, 0.0, upper[...])
    lower[...] = pltpu.roll(upper[...], 1, 1)
    partial_sum = storage + east[...] + north[...] + south[...] + upper[...] + lower[...]
    for b in range(BLOCKS):
        partial_sum = partial_sum + wells[b]
    rdiag[...] = partial_sum

    rates, strengths = [], []
    for k in range(FLOW_SWEEPS):
        if k == 0:

            @pl.when(jnp.logical_not(first))
            def _():
                tx_copy.wait_recv()

            rdiag[...] = 1.0 / (rdiag[...] + west[...])
        gather_wait(k, ag_recv.at[k])
        if k == 0:
            ids = ag0[:, :, 256:384]
            parts = ag0[:, :, 128:256]
            sums = ag0[:, :, 0:128]
            rate_at = iota((1, 256), 1)
            for b in range(BLOCKS):
                mask = jnp.where(ids == well_ids[b].reshape(1, 1, 1), 1.0, 0.0)
                masks[b] = mask
                strengths.append(total(jnp.sum(mask * parts, axis=0)))
                rates.append(
                    jnp.sum(
                        jnp.where(rate_at == well_ref[b : b + 1, :], rate_ref[...], 0.0),
                        axis=1,
                        keepdims=True,
                    )
                )
        else:
            sums = ag[k - 1]
        bottoms = [
            (rates[b] + total(jnp.sum(masks[b] * sums, axis=0))) / strengths[b]
            for b in range(BLOCKS)
        ]
        wait_halo(k)
        p = press[k]
        acc = base[...] + east[...] * halo_hi[k] + west[...] * halo_lo[k]
        acc = acc + north[...] * next_y(p) + south[...] * prev_y(p)
        acc = acc + upper[...] * pltpu.roll(p, NZ - 1, 1) + lower[...] * pltpu.roll(p, 1, 1)
        for b in range(BLOCKS):
            acc = acc + wells[b] * bottoms[b]
        new = acc * rdiag[...]
        if k < FLOW_SWEEPS - 1:
            press[k + 1] = new
            start_halo(k + 1)
            row = lanes(block_sums(k + 1))
            msg[k] = row
            ag[k, f] = row
            start_gather(k + 1)
        else:
            ppad[YS : YS + NY, :] = new
        if k == 1:
            @pl.when(has_lo)
            def _():
                for c in y_copies(True):
                    c.wait_recv()

            @pl.when(has_hi)
            def _():
                for c in y_copies(False):
                    c.wait_recv()

            own_u.wait()
            own_m.wait()

            @pl.when(g < NG - 1)
            def _():
                for c in x_copies(True):
                    c.start()

            @pl.when(g > 0)
            def _():
                for c in x_copies(False):
                    c.start()

    p_copy = pltpu.make_async_copy(ppad.at[pl.ds(YS, NY)], p_out.at[0], out_sem.at[0])
    p_copy.start()

    def window(t):
        return ppad.at[pl.ds(pl.multiple_of(t * YS, YS), YW)]

    own_window = pltpu.make_async_copy(window(d), pwin.at[HALO + d], pw_self)
    own_window.start()

    def send_own(i, carry):
        t = lax.rem(d + i, ND)
        pltpu.make_async_remote_copy(
            window(t), pwin.at[HALO + d], pw_send.at[0], pw_recv.at[0],
            device_id=(g, t), device_id_type=MESH,
        ).start()
        return carry

    lax.fori_loop(1, ND, send_own, 0)
    to_hi = jnp.logical_and(d >= XS - HALO, g < NG - 1)
    to_lo = jnp.logical_and(d < HALO, g > 0)

    @pl.when(to_hi)
    def _():
        def send(i, carry):
            t = lax.rem(d + i, ND)
            pltpu.make_async_remote_copy(
                window(t), pwin.at[d - (XS - HALO)], pw_send.at[1], pw_recv.at[1],
                device_id=(g + 1, t), device_id_type=MESH,
            ).start()
            return carry

        lax.fori_loop(0, ND, send, 0)

    @pl.when(to_lo)
    def _():
        def send(i, carry):
            t = lax.rem(d + i, ND)
            pltpu.make_async_remote_copy(
                window(t), pwin.at[HALO + XS + d], pw_send.at[2], pw_recv.at[2],
                device_id=(g - 1, t), device_id_type=MESH,
            ).start()
            return carry

        lax.fori_loop(0, ND, send, 0)

    def window_wait(count, sem):
        part = pwin.at[pl.ds(0, count)]
        pltpu.make_async_copy(part, part, sem).wait()

    @pl.when(g > 0)
    def _():
        for c in x_copies(True):
            c.wait_recv()

    @pl.when(g < NG - 1)
    def _():
        for c in x_copies(False):
            c.wait_recv()

    @pl.when(g < NG - 1)
    def _():
        for c in x_copies(True):
            c.wait_send()

    @pl.when(g > 0)
    def _():
        for c in x_copies(False):
            c.wait_send()

    row_y = iota((YW, NZ), 0) + (d - 1) * YS
    inside_y = jnp.logical_and(row_y >= 0, row_y < NY)

    def inside(i):
        x = g * XS - HALO + i
        return jnp.logical_and(inside_y, jnp.logical_and(x >= 0, x < NG * XS))

    def scale_plane(i, carry):
        gain[i] = jnp.where(inside(i), (-0.5 * BIOT * RELAX / 26.0), 0.0) / mod[i]
        return carry

    lax.fori_loop(1, XW - 1, scale_plane, 0)

    own_window.wait()
    window_wait(ND - 1, pw_recv.at[0])

    @pl.when(g > 0)
    def _():
        window_wait(HALO, pw_recv.at[1])

    @pl.when(g < NG - 1)
    def _():
        window_wait(HALO, pw_recv.at[2])

    def force_plane(i, carry):
        p = pwin[i]
        r = gain[i]
        force[0, i] = r * (pwin[i + 1] - pwin[i - 1])
        force[1, i] = r * (next_y(p) - prev_y(p))
        force[2, i] = r * (next_z(p) - prev_z(p))
        return carry

    lax.fori_loop(1, XW - 1, force_plane, 0)

    def z_stage(src, i):
        for c in range(3):
            v = src[c, i]
            hi, lo = next_z(v), prev_z(v)
            tzb[c, i] = v + hi + lo
            dzb[c, i] = hi - lo

    for s in range(MECH_SWEEPS):
        src, dst = (ua, ub) if s % 2 == 0 else (ub, ua)
        z_stage(src, s)
        z_stage(src, s + 1)

        def mech_plane(i, carry, src=src, dst=dst):
            z_stage(src, i + 1)
            ok = inside(i)
            alpha = jnp.where(ok, ALPHA, 0.0)
            beta = jnp.where(ok, BETA, 0.0)
            e = [
                COUPLE * (src[1, i + 1] - src[1, i - 1]),
                COUPLE * (src[0, i + 1] - src[0, i - 1] + dzb[2, i]),
                COUPLE * dzb[1, i],
            ]
            extra = [
                COUPLE * (dzb[2, i + 1] - dzb[2, i - 1]),
                None,
                COUPLE * (dzb[0, i + 1] - dzb[0, i - 1]),
            ]
            for c in range(3):
                box = tzb[c, i - 1] + tzb[c, i] + tzb[c, i + 1]
                r = box + next_y(box + e[c]) + prev_y(box - e[c])
                if extra[c] is not None:
                    r = r + extra[c]
                dst[c, i] = alpha * src[c, i] + beta * r + force[c, i]
            return carry

        lax.fori_loop(s + 1, XW - 1 - s, mech_plane, 0)

    final = ua if MECH_SWEEPS % 2 == 0 else ub
    u_copy = pltpu.make_async_copy(
        final.at[:, pl.ds(HALO, XS), pl.ds(YS, YS)], u_out, out_sem.at[1]
    )
    u_copy.start()

    rows = pl.ds(pl.multiple_of(d * YS, YS), YS)

    def strain_plane(i, carry):
        t = lax.rem(d + i, ND)
        x = t + HALO
        uy = final[1, x]
        uz = final[2, x, YS : 2 * YS, :]
        dx = final[0, x + 1, YS : 2 * YS, :] - final[0, x - 1, YS : 2 * YS, :]
        dy = (next_y(uy) - prev_y(uy))[YS : 2 * YS, :]
        strain[t] = 0.5 * (dx + dy + next_z(uz) - prev_z(uz))

        @pl.when(i > 0)
        def _():
            pltpu.make_async_remote_copy(
                strain.at[t], s_out.at[0, rows], st_send, st_recv,
                device_id=(g, t), device_id_type=MESH,
            ).start()

        return carry

    lax.fori_loop(0, ND, strain_plane, 0)
    own_strain = pltpu.make_async_copy(strain.at[d], s_out.at[0, rows], st_self)
    own_strain.start()

    @pl.when(jnp.logical_not(last))
    def _():
        tx_copy.wait_send()

    for k in range(FLOW_SWEEPS):
        wait_halo_send(k)
        gather_wait(k, ag_send.at[k])

    @pl.when(has_hi)
    def _():
        for c in y_copies(True):
            c.wait_send()

    @pl.when(has_lo)
    def _():
        for c in y_copies(False):
            c.wait_send()

    window_wait(ND - 1, pw_send.at[0])

    @pl.when(to_hi)
    def _():
        window_wait(ND, pw_send.at[1])

    @pl.when(to_lo)
    def _():
        window_wait(ND, pw_send.at[2])

    p_copy.wait()
    u_copy.wait()
    own_strain.wait()
    part = strain.at[pl.ds(0, ND - 1)]
    pltpu.make_async_copy(part, part, st_send).wait()
    pltpu.make_async_copy(part, part, st_recv).wait()


def body(
    pressure_old, strain_change, storage, trans_x, trans_y, trans_z, displacement_old, modulus,
    perf_cell, perf_well, perf_count, perf_index, well_rate,
):
    dma = pltpu.SemaphoreType.DMA
    vmem = lambda *shape: pltpu.VMEM(shape, F32)
    plane = (NY, NZ)
    window = (XW, YW, NZ)
    hbm = pl.BlockSpec(memory_space=pl.ANY)
    local = pl.BlockSpec(memory_space=pltpu.VMEM)
    return pl.pallas_call(
        kernel,
        name="poro_step",
        out_shape=(
            jax.ShapeDtypeStruct((1, NY, NZ), F32),
            jax.ShapeDtypeStruct((3, XS, YS, NZ), F32),
            jax.ShapeDtypeStruct((1, NY, NZ), F32),
        ),
        in_specs=[hbm] * 8 + [local] * 5,
        out_specs=(hbm, hbm, hbm),
        scratch_shapes=[
            vmem(FLOW_SWEEPS, *plane),
            vmem(*plane),
            vmem(*plane),
            vmem(*plane),
            vmem(*plane),
            vmem(*plane),
            vmem(*plane),
            vmem(*plane),
            vmem(*plane),
            vmem(BLOCKS, *plane),
            vmem(FLOW_SWEEPS, *plane),
            vmem(FLOW_SWEEPS, *plane),
            vmem(1, 384),
            vmem(FLOW_SWEEPS - 1, 1, 128),
            vmem(NF, 1, 384),
            vmem(FLOW_SWEEPS - 1, NF, 1, 128),
            vmem(BLOCKS, NF, 1, 128),
            vmem(NY + 2 * YS, NZ),
            vmem(*window),
            vmem(3, *window),
            vmem(3, *window),
            vmem(*window),
            vmem(*window),
            vmem(3, *window),
            vmem(3, *window),
            vmem(3, *window),
            vmem(XS, YS, NZ),
            dma((6,)),
            dma((2,)),
            dma((2, FLOW_SWEEPS)),
            dma((2, FLOW_SWEEPS)),
            dma,
            dma,
            dma((FLOW_SWEEPS,)),
            dma((FLOW_SWEEPS,)),
            dma((2, 2)),
            dma((2, 2)),
            dma((2, 2)),
            dma((2, 2)),
            dma((3,)),
            dma((3,)),
            dma,
            dma,
            dma,
            dma,
            dma((2,)),
        ],
        compiler_params=pltpu.CompilerParams(
            collective_id=0, has_side_effects=True, vmem_limit_bytes=48 << 20
        ),
    )(
        pressure_old, strain_change, storage, trans_x, trans_y, trans_z, displacement_old, modulus,
        perf_cell, perf_well.reshape(BLOCKS, 1), perf_count.reshape(BLOCKS, 1), perf_index,
        well_rate.reshape(1, -1),
    )


def solution(mesh):
    flow = P(("grp", "dev"), None, None)
    slabs = P(None, "grp", "dev", None)
    return jax.shard_map(
        body,
        mesh=mesh,
        in_specs=(
            flow, flow, flow, flow, flow, flow, slabs, P("grp", "dev", None),
            P(("grp", "dev"), None), P(("grp", "dev")), P(("grp", "dev")), P(("grp", "dev"), None), P(),
        ),
        out_specs=(flow, slabs, flow),
        check_vma=False,
    )
```

time: 592 us -> 166 us (0.28); the launches traced: 581 us -> 165 us
  blocking collectives: 314 us -> 0 us
  starting transfers between devices: 157 us -> 0 us
  Pallas kernels: 0 us -> 153 us
  other arithmetic: 45.5 us -> 0 us
  waiting for transfers between devices: 27 us -> 0 us
  local copies, waits for them, and re-layouts: 35.2 us -> 11.5 us
    psum x4 -> x0, blocking collectives: 261 us -> none  [body(): well_sum, strength = lax.psum((well_part, strength_part), ('grp', 'dev'))]
    pallas_call x0 -> x1, Pallas kernels: none -> 153 us  [body(): pl.pallas_call(kernel, name='poro_step', out_shape=(jax.ShapeDtypeStruct(...]
    ppermute x41 -> x0, starting transfers between devices: 152 us -> none  [the longest x21 86.1 us: padded_2(): lax.ppermute(lax.slice_in_dim(block, block.shape[dim] - width, None, axis...]
    all_to_all x1 -> x0, blocking collectives: 53 us -> none  [body(): lax.all_to_all(strain_mech, 'dev', split_axis=0, concat_axis=1, tiled=True)]
    ppermute x41 -> x0, waiting for transfers between devices: 19 us -> none  [the longest x21 16.4 us: padded_2(): lax.ppermute(lax.slice_in_dim(block, block.shape[dim] - width, None, axis...]
    scatter-add x5 -> x0, other arithmetic: 18.3 us -> none  [the longest x4 15 us: body(): inflow = jnp.zeros((cell_count,), jnp.float32).at[flat_cell].add((weight...]
    gather x4 -> x0, local copies, waits for them, and re-layouts: 12.6 us -> none  [body(): sampled = pressure.reshape(-1)[flat_cell].reshape(weight.shape)]
    add x36 -> x0, other arithmetic: 12.1 us -> none  [the longest x6 4.3 us: stiffness(): column_sum = field + above_z(field) + below_z(field)]
  transfers between devices with their start and end apart: 42 -> 0, of which waited for: 22 -> 0; matrix products, arithmetic and copies ran while one was open for 9% -> 0% of each run, Pallas kernels for 0% -> 0%
where the time goes in v1:
time: 166 us; the launch traced here: 165 us
  Pallas kernels  153 us (92%)
  local copies, waits for them, and re-layouts  11.5 us (7%)
    pallas_call x1, Pallas kernels, body(): pl.pallas_call(kernel, name='poro_step', out_shape=(jax.ShapeDtypeStruct(...  153 us
    unnamed x29, local copies, waits for them, and re-layouts  11.3 us

profile of v1, /device:TPU:1, one launch (start us, length us, event | category | flops | bytes accessed | tf_op | source)
XLA Modules:
  0.0 165.1 jit_solution(10352121395760655044)
XLA Ops:
  0.6 0.0 copy-start.11
  0.6 0.0 copy-start.12
  0.7 0.6 copy-done.11
  1.3 0.0 copy-start.8
  1.3 0.0 copy-start.9
  1.3 0.1 copy.16.well_ref
  1.4 0.0 copy-done.12
  1.4 0.0 copy-start.10
  1.4 0.1 copy.17.cnt_ref
  1.5 0.5 copy-done.8
  2.0 0.0 copy-done.9
  2.0 0.1 copy-done.10
  2.1 0.0 copy-start
  2.1 1.1 copy-done
  3.2 0.0 copy-start.1
  3.2 0.9 copy-done.1
  4.2 0.0 copy-start.2
  4.2 0.9 copy-done.2
  5.1 0.0 copy-start.3
  5.1 0.9 copy-done.3
  6.1 0.0 copy-start.4
  6.1 0.9 copy-done.4
  7.0 0.0 copy-start.5
  7.0 0.9 copy-done.5
  8.0 0.0 copy-start.6
  8.0 0.9 copy-done.6
  8.9 0.0 copy-start.7
  8.9 0.9 copy-done.7
  9.9 153.0 %poro_step.1 = (f32[1,256,256]{2,1,0:T(8,128)S(1)}, f32[3,32,8,256]{3,2,1,0:T(8,128)S(1)}, f32[1,256,256]{2,1,0:T(8,128)S(1)}) custom-call(f32[1,256,256]{2,1,0:T(8,128)S(1)} %copy-done.1, f32[1,256,256]{2,1,0:T(8,128)S(1)} %copy-done.2, f32[1,256,256]{2,1,0:T(8,128)S(1)} %copy-done.3, f32[1,256,256]{2,1,0:T(8,128)S(1)} %copy-done.4, ...), custom_call_target="tpu_custom_call" | custom-call | tf_op jit(solution)/shard_map/poro_step/pallas_call | solution.py:603
  162.8 0.7 copy.21
  163.5 0.9 copy.22
  164.4 0.7 copy.23
Async XLA Ops:
  0.6 0.7 copy-start.11
  0.6 0.7 copy-start.12
  1.3 0.7 copy-start.8
  1.3 0.7 copy-start.9
  1.4 0.7 copy-start.10
  2.1 1.1 copy-start
  3.2 0.9 copy-start.1
  4.2 0.9 copy-start.2
  5.1 0.9 copy-start.3
  6.1 0.9 copy-start.4
  7.0 0.9 copy-start.5
  8.0 0.9 copy-start.6
  8.9 0.9 copy-start.7

commit v2 on v1

v2 whole, which is shorter than its diff:
```python
import functools

import jax
import jax.numpy as jnp
from jax import lax
from jax.experimental import pallas as pl
from jax.experimental.pallas import tpu as pltpu
from jax.sharding import PartitionSpec as P

MESH = pl.DeviceIdType.MESH
F32 = jnp.float32

FLOW_SWEEPS = 4
MECH_SWEEPS = 6
BIOT = 0.8
RELAX = 0.6
COUPLE = 0.375

NG, ND = 4, 32
NF = NG * ND
NY, NZ = 256, 256
XS, YS = 32, 8
HALO = MECH_SWEEPS + 1
CH, SL = 8, 6
XW = CH * SL
YW = 3 * YS
BLOCKS = 4

ALPHA = 1.0 - RELAX * 27.0 / 26.0
BETA = RELAX / 26.0


def iota(shape, dim):
    return lax.broadcasted_iota(jnp.int32, shape, dim)


def next_z(v):
    n = v.shape[-1]
    return jnp.where(iota(v.shape, 1) == n - 1, 0.0, pltpu.roll(v, n - 1, 1))


def prev_z(v):
    return jnp.where(iota(v.shape, 1) == 0, 0.0, pltpu.roll(v, 1, 1))


def next_y(v):
    return pltpu.roll(v, v.shape[0] - 1, 0)


def prev_y(v):
    return pltpu.roll(v, 1, 0)


def extend(slots):
    return [pltpu.roll(slots[-1], 1, 0)] + slots + [pltpu.roll(slots[0], CH - 1, 0)]


def total(v):
    return jnp.sum(jnp.sum(v, axis=0, keepdims=True), axis=1, keepdims=True)


def kernel(
    p0_h, sc_h, st_h, tx_h, ty_h, tz_h, u_h, mod_h, cell_h, well_h, cnt_h, idx_h, rate_h,
    p_out, u_out, s_out,
    cell_ref, well_ref, cnt_ref, idx_ref, rate_ref,
    press, base, east, west, north, south, upper, lower, rdiag, wells, halo_lo, halo_hi,
    msg, ag0, ag, masks,
    ppad, nat, pwin, ua, ub, gain, force, xsum, shear, dy_z, dz_z, dx_z, betas, strain,
    small_sem, load_sem, uload_sem, halo_send, halo_recv, tx_send, tx_recv, ag_send, ag_recv,
    usend, urecv, xsend, xrecv, relay_sem, pw_send, pw_recv, pw_self, st_send, st_recv, st_self,
    out_sem,
):
    g = lax.axis_index("grp")
    d = lax.axis_index("dev")
    f = g * ND + d
    first, last = f == 0, f == NF - 1
    has_lo, has_hi = d > 0, d < ND - 1
    has_west, has_east = g > 0, g < NG - 1

    def flow_dev(k):
        return (k // ND, lax.rem(k, ND))

    after, before = flow_dev(lax.rem(f + 1, NF)), flow_dev(lax.rem(f + NF - 1, NF))

    small_loads = [
        pltpu.make_async_copy(src, dst, small_sem.at[i])
        for i, (src, dst) in enumerate(
            [
                (cell_h, cell_ref),
                (well_h, well_ref),
                (cnt_h, cnt_ref),
                (idx_h, idx_ref),
                (rate_h, rate_ref),
            ]
        )
    ]
    plane_loads = [
        pltpu.make_async_copy(src.at[0], dst, load_sem.at[i])
        for i, (src, dst) in enumerate(
            [
                (p0_h, press.at[0]),
                (sc_h, base),
                (st_h, rdiag),
                (tx_h, east),
                (ty_h, north),
                (tz_h, upper),
            ]
        )
    ]
    own_u = pltpu.make_async_copy(
        u_h, nat.at[pl.ds(0, 3), pl.ds(HALO, XS), pl.ds(YS, YS)], uload_sem.at[0]
    )
    own_m = pltpu.make_async_copy(
        mod_h, nat.at[3, pl.ds(HALO, XS), pl.ds(YS, YS)], uload_sem.at[1]
    )
    for c in small_loads + plane_loads + [own_u, own_m]:
        c.start()

    def fill(planes, rows):
        n, m = planes.stop - planes.start, rows.stop - rows.start
        nat[0:3, planes, rows, :] = jnp.zeros((3, n, m, NZ), F32)
        nat[3, planes, rows, :] = jnp.ones((n, m, NZ), F32)

    own_planes, all_rows = slice(HALO, HALO + XS), slice(0, YW)
    fill(slice(2 * HALO + XS, XW), all_rows)
    pwin[...] = jnp.zeros(pwin.shape, F32)

    @pl.when(d == 0)
    def _():
        fill(own_planes, slice(0, YS))

    @pl.when(d == ND - 1)
    def _():
        fill(own_planes, slice(2 * YS, YW))

    @pl.when(g == 0)
    def _():
        fill(slice(0, HALO), all_rows)

    @pl.when(g == NG - 1)
    def _():
        fill(slice(HALO + XS, 2 * HALO + XS), all_rows)

    barrier = pltpu.get_barrier_semaphore()

    def greet(i, carry):
        pl.semaphore_signal(
            barrier, inc=1, device_id=flow_dev(lax.rem(f + i, NF)), device_id_type=MESH
        )
        return carry

    lax.fori_loop(1, NF, greet, 0)

    @pl.when(first)
    def _():
        halo_lo[...] = jnp.zeros(halo_lo.shape, F32)
        west[...] = jnp.zeros((NY, NZ), F32)

    @pl.when(last)
    def _():
        halo_hi[...] = jnp.zeros(halo_hi.shape, F32)

    ppad[0:YS, :] = jnp.zeros((YS, NZ), F32)
    ppad[NY + YS :, :] = jnp.zeros((YS, NZ), F32)
    for i in range(SL):
        x = iota((CH, NZ), 0) * SL + i + g * XS - HALO
        betas[i] = jnp.where(jnp.logical_and(x >= 0, x < NG * XS), BETA, 0.0)

    for c in small_loads:
        c.wait()
    lane = iota((1, 128), 1)
    weight_sums = []
    for b in range(BLOCKS):
        live = lane < cnt_ref[b]
        weight = jnp.where(live, idx_ref[b : b + 1, :], 0.0)
        cell = cell_ref[b : b + 1, :]
        row, col = cell // NZ, lax.rem(cell, NZ)
        at_row = iota((NY, 128), 0) == row
        at_col = jnp.where(iota((NZ, 128), 0) == col, 1.0, 0.0).astype(jnp.bfloat16)
        rest = weight
        plane = jnp.zeros((NY, NZ), F32)
        for _ in range(3):
            part = rest.astype(jnp.bfloat16)
            rest = rest - part.astype(F32)
            spread = jnp.where(at_row, part.astype(F32), 0.0).astype(jnp.bfloat16)
            plane = plane + lax.dot_general(
                spread, at_col, (((1,), (1,)), ((), ())), preferred_element_type=F32
            )
        wells[b] = plane
        weight_sums.append(jnp.sum(weight, axis=1, keepdims=True))

    for c in plane_loads:
        c.wait()

    def halo_copies(k):
        up = pltpu.make_async_remote_copy(
            press.at[k], halo_lo.at[k], halo_send.at[0, k], halo_recv.at[0, k],
            device_id=after, device_id_type=MESH,
        )
        down = pltpu.make_async_remote_copy(
            press.at[k], halo_hi.at[k], halo_send.at[1, k], halo_recv.at[1, k],
            device_id=before, device_id_type=MESH,
        )
        return up, down

    tx_copy = pltpu.make_async_remote_copy(
        tx_h.at[0], west, tx_send, tx_recv, device_id=after, device_id_type=MESH
    )

    def start_halo(k):
        up, down = halo_copies(k)

        @pl.when(jnp.logical_not(last))
        def _():
            up.start()

        @pl.when(jnp.logical_not(first))
        def _():
            down.start()

    def wait_halo(k):
        up, down = halo_copies(k)

        @pl.when(jnp.logical_not(first))
        def _():
            up.wait_recv()

        @pl.when(jnp.logical_not(last))
        def _():
            down.wait_recv()

    def wait_halo_send(k):
        up, down = halo_copies(k)

        @pl.when(jnp.logical_not(last))
        def _():
            up.wait_send()

        @pl.when(jnp.logical_not(first))
        def _():
            down.wait_send()

    def lanes(values):
        out = jnp.zeros((1, 128), F32)
        for j, v in enumerate(values):
            out = jnp.where(lane == j, v, out)
        return out

    def block_sums(p):
        return lanes([total(wells[b] * p) for b in range(BLOCKS)])

    core, z_lo = lax.rem(g, 2), g // 2
    z_hi, phys_x, phys_y = d // 16, lax.rem(d // 4, 4), lax.rem(d, 4)
    spots = sorted(
        ((x, y) for x in range(4) for y in range(4)),
        key=lambda o: -(min(o[0], 4 - o[0]) + min(o[1], 4 - o[1])),
    )

    def gather_refs(k):
        if k == 0:
            return msg.at[pl.ds(0, 3), pl.ds(0, 1)], lambda r, n: ag0.at[:, pl.ds(r, n)]
        return msg.at[2 + k, pl.ds(0, 1)], lambda r, n: ag.at[k - 1, pl.ds(r, n)]

    def start_gather(k):
        src, dst = gather_refs(k)
        for ox, oy in spots:
            x, y = lax.rem(phys_x + ox, 4), lax.rem(phys_y + oy, 4)

            def send(i, carry, x=x, y=y):
                j = 7 - i
                zh = lax.rem(z_hi + j // 4, 2)
                zl = lax.rem(z_lo + lax.rem(j // 2, 2), 2)
                c = lax.rem(core + lax.rem(j, 2), 2)
                pltpu.make_async_remote_copy(
                    src, dst(f, 1), ag_send.at[k], ag_recv.at[k],
                    device_id=(zl * 2 + c, zh * 16 + x * 4 + y), device_id_type=MESH,
                ).start()
                return carry

            lax.fori_loop(0, 7 if ox == 0 and oy == 0 else 8, send, 0)

    def gather_wait(k, sem):
        part = gather_refs(k)[1](0, NF - 1)
        pltpu.make_async_copy(part, part, sem).wait()

    def y_copies(a):
        src = mod_h if a == 3 else u_h.at[a]
        out = []
        for s, (k, at) in enumerate([(lax.rem(d + 1, ND), 0), (lax.rem(d + ND - 1, ND), 2 * YS)]):
            out.append(
                pltpu.make_async_remote_copy(
                    src, nat.at[a, pl.ds(HALO, XS), pl.ds(at, YS)],
                    usend.at[s, a], urecv.at[s, a], device_id=(g, k), device_id_type=MESH,
                )
            )
        return out

    def x_copies(a):
        out = []
        for s, (k, at, to) in enumerate(
            [(lax.rem(g + 1, NG), XS, 0), (lax.rem(g + NG - 1, NG), HALO, HALO + XS)]
        ):
            out.append(
                pltpu.make_async_remote_copy(
                    nat.at[a, pl.ds(at, HALO)], nat.at[a, pl.ds(to, HALO)],
                    xsend.at[s, a], xrecv.at[s, a], device_id=(k, d), device_id_type=MESH,
                )
            )
        return out

    def start_pair(copies, to_up, to_down):
        @pl.when(to_up)
        def _():
            copies[0].start()

        @pl.when(to_down)
        def _():
            copies[1].start()

    def recv_pair(copies, to_up, to_down):
        @pl.when(to_down)
        def _():
            copies[0].wait_recv()

        @pl.when(to_up)
        def _():
            copies[1].wait_recv()

    def send_pair(copies, to_up, to_down):
        @pl.when(to_up)
        def _():
            copies[0].wait_send()

        @pl.when(to_down)
        def _():
            copies[1].wait_send()

    def pass_on(a):
        recv_pair(y_copies(a), has_hi, has_lo)
        start_pair(x_copies(a), has_east, has_west)

    def relay_copies(a):
        dst = gain if a == 3 else ua.at[a]
        return [
            pltpu.make_async_copy(
                nat.at[a, pl.ds(c * SL, SL)], dst.at[:, :, c], relay_sem.at[a, c]
            )
            for c in range(CH)
        ]

    def relay(a):
        recv_pair(x_copies(a), has_east, has_west)
        send_pair(x_copies(a), has_east, has_west)
        for c in relay_copies(a):
            c.start()

    pl.semaphore_wait(barrier, NF - 1)

    @pl.when(jnp.logical_not(last))
    def _():
        tx_copy.start()

    start_halo(0)
    well_ids = [well_ref[b].astype(F32) for b in range(BLOCKS)]
    msg[0, 0:1] = block_sums(press[0])
    msg[1, 0:1] = lanes(weight_sums)
    msg[2, 0:1] = jnp.where(lane < BLOCKS, lanes(well_ids), -1.0)
    for j in range(3):
        ag0[j, pl.ds(f, 1), :] = msg[j, 0:1]
    start_gather(0)
    start_pair(y_copies(3), has_hi, has_lo)

    p0 = press[0]
    storage = rdiag[...]
    base[...] = storage * p0 - BIOT * base[...]
    east[...] = jnp.where(last, 0.0, east[...])
    north[...] = jnp.where(iota((NY, NZ), 0) == NY - 1, 0.0, north[...])
    south[...] = prev_y(north[...])
    upper[...] = jnp.where(iota((NY, NZ), 1) == NZ - 1, 0.0, upper[...])
    lower[...] = pltpu.roll(upper[...], 1, 1)
    partial_sum = storage + east[...] + north[...] + south[...] + upper[...] + lower[...]
    for b in range(BLOCKS):
        partial_sum = partial_sum + wells[b]
    rdiag[...] = partial_sum
    own_u.wait()
    own_m.wait()

    rates, strengths = [], []
    for k in range(FLOW_SWEEPS):
        if k == 0:

            @pl.when(jnp.logical_not(first))
            def _():
                tx_copy.wait_recv()

            rdiag[...] = 1.0 / (rdiag[...] + west[...])
        wait_halo(k)
        order = [3, 0, 1, 2]
        pass_on(order[k])
        if k < 3:
            start_pair(y_copies(order[k + 1]), has_hi, has_lo)
        if k > 0:
            relay(order[k - 1])
        gather_wait(k, ag_recv.at[k])
        if k == 0:
            sums = ag0[0]
            rate_at = iota((1, 256), 1)
            for b in range(BLOCKS):
                mask = jnp.where(ag0[2] == well_ids[b], 1.0, 0.0)
                masks[b] = mask
                strengths.append(total(mask * ag0[1]))
                rates.append(
                    jnp.sum(
                        jnp.where(rate_at == well_ref[b], rate_ref[...], 0.0),
                        axis=1,
                        keepdims=True,
                    )
                )
        else:
            sums = ag[k - 1]
        bottoms = [(rates[b] + total(masks[b] * sums)) / strengths[b] for b in range(BLOCKS)]
        p = press[k]
        acc = base[...] + east[...] * halo_hi[k] + west[...] * halo_lo[k]
        acc = acc + north[...] * next_y(p) + south[...] * prev_y(p)
        acc = acc + upper[...] * pltpu.roll(p, NZ - 1, 1) + lower[...] * pltpu.roll(p, 1, 1)
        for b in range(BLOCKS):
            acc = acc + wells[b] * bottoms[b]
        new = acc * rdiag[...]
        if k < FLOW_SWEEPS - 1:
            press[k + 1] = new
            start_halo(k + 1)
            row = block_sums(new)
            msg[3 + k, 0:1] = row
            ag[k, pl.ds(f, 1), :] = row
            start_gather(k + 1)
        else:
            ppad[YS : YS + NY, :] = new

    def window(t):
        return ppad.at[pl.ds(pl.multiple_of(t * YS, YS), YW)]

    def place(x):
        return pwin.at[lax.rem(x, SL), :, x // SL]

    own_window = pltpu.make_async_copy(window(d), place(HALO + d), pw_self)
    own_window.start()

    def spread(first_step, x, target, j):
        def send(i, carry):
            t = lax.rem(d + i, ND)
            pltpu.make_async_remote_copy(
                window(t), place(x), pw_send.at[j], pw_recv.at[j],
                device_id=(target, t), device_id_type=MESH,
            ).start()
            return carry

        lax.fori_loop(first_step, ND, send, 0)

    spread(1, HALO + d, g, 0)
    to_hi = jnp.logical_and(d >= XS - HALO, has_east)
    to_lo = jnp.logical_and(d < HALO, has_west)

    @pl.when(to_hi)
    def _():
        spread(0, d - (XS - HALO), g + 1, 1)

    @pl.when(to_lo)
    def _():
        spread(0, HALO + XS + d, g - 1, 2)

    p_copy = pltpu.make_async_copy(ppad.at[pl.ds(YS, NY)], p_out.at[0], out_sem.at[0])
    p_copy.start()

    def window_wait(count, sem):
        part = nat.at[0, pl.ds(0, count)]
        pltpu.make_async_copy(part, part, sem).wait()

    relay(2)
    for c in relay_copies(3):
        c.wait()

    def gain_row(y, carry):
        gy = (d - 1) * YS + y
        inside = jnp.logical_and(gy >= 0, gy < NY)
        scale = jnp.where(inside, -0.5 * BIOT / BETA * RELAX / 26.0, 0.0)
        for i in range(SL):
            gain[i, y] = scale * betas[i] / gain[i, y]
        return carry

    lax.fori_loop(2, YW - 2, gain_row, 0)
    for a in range(3):
        for c in relay_copies(a):
            c.wait()

    own_window.wait()
    window_wait(ND - 1, pw_recv.at[0])

    @pl.when(has_west)
    def _():
        window_wait(HALO, pw_recv.at[1])

    @pl.when(has_east)
    def _():
        window_wait(HALO, pw_recv.at[2])

    def force_row(y, carry):
        p = extend([pwin[i, y] for i in range(SL)])
        for i in range(SL):
            r = gain[i, y]
            force[0, i, y] = r * (p[i + 2] - p[i])
            force[1, i, y] = r * (pwin[i, y + 1] - pwin[i, y - 1])
            force[2, i, y] = r * (next_z(p[i + 1]) - prev_z(p[i + 1]))
        return carry

    lax.fori_loop(2, YW - 2, force_row, 0)

    for s in range(MECH_SWEEPS):
        src, dst = (ua, ub) if s % 2 == 0 else (ub, ua)
        y0, y1 = 2 + s, YW - 2 - s

        def row_values(y, src=src):
            tz, dz = [], []
            for c in range(3):
                t, q = [], []
                for i in range(SL):
                    v = src[c, i, y]
                    hi, lo = next_z(v), prev_z(v)
                    t.append(v + hi + lo)
                    q.append(hi - lo)
                tz.append(extend(t))
                dz.append(q)
            sums = []
            for t in tz:
                r = []
                for i in range(0, SL, 2):
                    pair = t[i + 1] + t[i + 2]
                    r += [t[i] + pair, pair + t[i + 3]]
                sums.append(r)
            ux = extend([src[0, i, y] for i in range(SL)])
            dx = extend(dz[0])
            along_y = [ux[i + 2] - ux[i] + dz[2][i] for i in range(SL)]
            cross = [dx[i + 2] - dx[i] for i in range(SL)]
            return sums, along_y, dz[1], dz[2], cross

        def row_store(y, values):
            sums, along_y, dzy, dzz, cross = values
            for i in range(SL):
                for c in range(3):
                    xsum[c, i, y] = sums[c][i]
                shear[i, y] = along_y[i]
                dy_z[i, y] = dzy[i]
                dz_z[i, y] = dzz[i]
                dx_z[i, y] = cross[i]

        def combine(y, src=src, dst=dst):
            gy = (d - 1) * YS + y
            inside = jnp.logical_and(gy >= 0, gy < NY).astype(F32)
            along_x = extend([src[1, i, y + 1] - src[1, i, y - 1] + dz_z[i, y] for i in range(SL)])
            for i in range(SL):
                beta = betas[i] * inside
                mixed = [
                    along_x[i + 2] - along_x[i],
                    shear[i, y + 1] - shear[i, y - 1],
                    dx_z[i, y] + dy_z[i, y + 1] - dy_z[i, y - 1],
                ]
                for c in range(3):
                    box = xsum[c, i, y - 1] + xsum[c, i, y] + xsum[c, i, y + 1]
                    r = box + COUPLE * mixed[c] + (ALPHA / BETA) * src[c, i, y]
                    dst[c, i, y] = beta * r + force[c, i, y]

        for y in (y0 - 1, y0, y0 + 1):
            row_store(y, row_values(y))

        def mech_row(y, carry, y1=y1):
            ahead = jnp.minimum(y + 2, y1)
            values = row_values(ahead)
            combine(y)
            row_store(ahead, values)
            return carry

        lax.fori_loop(y0, y1, mech_row, 0, unroll=2)

    final = ua if MECH_SWEEPS % 2 == 0 else ub

    def strain_row(y, carry):
        ux = extend([final[0, i, y] for i in range(SL)])
        for i in range(SL):
            uz = final[2, i, y]
            div = ux[i + 2] - ux[i] + final[1, i, y + 1] - final[1, i, y - 1]
            strain[i, y - YS] = 0.5 * (div + next_z(uz) - prev_z(uz))
        return carry

    lax.fori_loop(YS, 2 * YS, strain_row, 0)
    rows = pl.ds(pl.multiple_of(d * YS, YS), YS)

    def strain_of(t):
        x = t + HALO
        return strain.at[lax.rem(x, SL), :, x // SL]

    def send_strain(i, carry):
        t = lax.rem(d + i, ND)
        pltpu.make_async_remote_copy(
            strain_of(t), s_out.at[0, rows], st_send, st_recv,
            device_id=(g, t), device_id_type=MESH,
        ).start()
        return carry

    lax.fori_loop(1, ND, send_strain, 0)
    own_strain = pltpu.make_async_copy(strain_of(d), s_out.at[0, rows], st_self)
    own_strain.start()
    u_copies = []
    for c in range(CH):
        lo, hi = max(c * SL, HALO), min((c + 1) * SL, HALO + XS)
        if lo < hi:
            u_copies.append(
                pltpu.make_async_copy(
                    final.at[:, pl.ds(lo - c * SL, hi - lo), pl.ds(YS, YS), c],
                    u_out.at[:, pl.ds(lo - HALO, hi - lo)],
                    out_sem.at[1 + c],
                )
            )
    for c in u_copies:
        c.start()

    @pl.when(jnp.logical_not(last))
    def _():
        tx_copy.wait_send()

    for k in range(FLOW_SWEEPS):
        wait_halo_send(k)
        gather_wait(k, ag_send.at[k])
    for a in range(4):
        send_pair(y_copies(a), has_hi, has_lo)
    window_wait(ND - 1, pw_send.at[0])

    @pl.when(to_hi)
    def _():
        window_wait(ND, pw_send.at[1])

    @pl.when(to_lo)
    def _():
        window_wait(ND, pw_send.at[2])

    p_copy.wait()
    for c in u_copies:
        c.wait()
    own_strain.wait()
    part = ppad.at[pl.ds(0, (ND - 1) * YS)]
    pltpu.make_async_copy(part, part, st_send).wait()
    pltpu.make_async_copy(part, part, st_recv).wait()


def body(
    pressure_old, strain_change, storage, trans_x, trans_y, trans_z, displacement_old, modulus,
    perf_cell, perf_well, perf_count, perf_index, well_rate,
):
    dma = pltpu.SemaphoreType.DMA
    vmem = lambda *shape: pltpu.VMEM(shape, F32)
    plane = (NY, NZ)
    slabs = (SL, YW, CH, NZ)
    hbm = pl.BlockSpec(memory_space=pl.ANY)
    return pl.pallas_call(
        kernel,
        name="poro_step",
        out_shape=(
            jax.ShapeDtypeStruct((1, NY, NZ), F32),
            jax.ShapeDtypeStruct((3, XS, YS, NZ), F32),
            jax.ShapeDtypeStruct((1, NY, NZ), F32),
        ),
        in_specs=[hbm] * 13,
        out_specs=(hbm, hbm, hbm),
        scratch_shapes=[
            pltpu.VMEM((BLOCKS, 128), jnp.int32),
            pltpu.SMEM((BLOCKS,), jnp.int32),
            pltpu.SMEM((BLOCKS,), jnp.int32),
            vmem(BLOCKS, 128),
            vmem(1, 256),
            vmem(FLOW_SWEEPS, *plane),
            vmem(*plane),
            vmem(*plane),
            vmem(*plane),
            vmem(*plane),
            vmem(*plane),
            vmem(*plane),
            vmem(*plane),
            vmem(*plane),
            vmem(BLOCKS, *plane),
            vmem(FLOW_SWEEPS, *plane),
            vmem(FLOW_SWEEPS, *plane),
            vmem(3 + FLOW_SWEEPS - 1, 8, 128),
            vmem(3, NF, 128),
            vmem(FLOW_SWEEPS - 1, NF, 128),
            vmem(BLOCKS, NF, 128),
            vmem(NY + 2 * YS, NZ),
            vmem(4, XW, YW, NZ),
            vmem(*slabs),
            vmem(3, *slabs),
            vmem(3, *slabs),
            vmem(*slabs),
            vmem(3, *slabs),
            vmem(3, *slabs),
            vmem(*slabs),
            vmem(*slabs),
            vmem(*slabs),
            vmem(*slabs),
            vmem(SL, CH, NZ),
            vmem(SL, YS, CH, NZ),
            dma((5,)),
            dma((6,)),
            dma((2,)),
            dma((2, FLOW_SWEEPS)),
            dma((2, FLOW_SWEEPS)),
            dma,
            dma,
            dma((FLOW_SWEEPS,)),
            dma((FLOW_SWEEPS,)),
            dma((2, 4)),
            dma((2, 4)),
            dma((2, 4)),
            dma((2, 4)),
            dma((4, CH)),
            dma((3,)),
            dma((3,)),
            dma,
            dma,
            dma,
            dma,
            dma((1 + CH,)),
        ],
        compiler_params=pltpu.CompilerParams(
            collective_id=0, has_side_effects=True, vmem_limit_bytes=62 << 20
        ),
    )(
        pressure_old, strain_change, storage, trans_x, trans_y, trans_z, displacement_old, modulus,
        perf_cell, perf_well, perf_count, perf_index,
        well_rate.reshape(1, -1),
    )


def solution(mesh):
    flow = P(("grp", "dev"), None, None)
    slabs = P(None, "grp", "dev", None)
    return jax.shard_map(
        body,
        mesh=mesh,
        in_specs=(
            flow, flow, flow, flow, flow, flow, slabs, P("grp", "dev", None),
            P(("grp", "dev"), None), P(("grp", "dev")), P(("grp", "dev")), P(("grp", "dev"), None), P(),
        ),
        out_specs=(flow, slabs, flow),
        check_vma=False,
    )
```

time: 166 us -> 131 us (0.79)
  Pallas kernels: 153 us -> 125 us
  local copies, waits for them, and re-layouts: 11.5 us -> 4.48 us
    pallas_call x1, Pallas kernels: 153 us -> 125 us  [body(): pl.pallas_call(kernel, name='poro_step', out_shape=(jax.ShapeDtypeStruct(...]
    unnamed x29 -> x5, local copies, waits for them, and re-layouts: 11.3 us -> 4.48 us
where the time goes in v2:
time: 131 us
  Pallas kernels  125 us (95%)
  local copies, waits for them, and re-layouts  4.48 us (3%)
    pallas_call x1, Pallas kernels, body(): pl.pallas_call(kernel, name='poro_step', out_shape=(jax.ShapeDtypeStruct(...  125 us
    unnamed x5, local copies, waits for them, and re-layouts  4.48 us

profile of v2, /device:TPU:1, one launch (start us, length us, event | category | flops | bytes accessed | tf_op | source)
XLA Modules:
  0.0 130.6 jit_solution(7652704297108486257)
XLA Ops:
  0.6 125.4 %poro_step.1 = (f32[1,256,256]{2,1,0:T(8,128)}, f32[3,32,8,256]{3,2,1,0:T(8,128)}, f32[1,256,256]{2,1,0:T(8,128)}) custom-call(f32[1,256,256]{2,1,0:T(8,128)} %p0_h.1, f32[1,256,256]{2,1,0:T(8,128)} %sc_h.1, f32[1,256,256]{2,1,0:T(8,128)} %st_h.1, f32[1,256,256]{2,1,0:T(8,128)} %tx_h.1, f32[1,256,256]{2,1,0:T(8,128)} %ty_h.1, f32[1,256,256]{2,1,0:T(8,128)} %tz_h.1, ...), custom_call_target="tpu_custom_call" | custom-call | tf_op jit(solution)/shard_map/poro_step/pallas_call | solution.py:662
  126.1 1.7 %copy.19 = f32[1,256,256]{2,1,0:T(8,128)} copy(f32[1,256,256]{2,1,0:T(8,128)} %get-tuple-element.6) | data formatting | bytes 524288
  127.7 0.0 copy-start
  127.7 2.1 %copy.20 = f32[3,32,8,256]{3,2,1,0:T(8,128)} copy(f32[3,32,8,256]{3,2,1,0:T(8,128)} %get-tuple-element.7) | data formatting | bytes 1572864
  129.9 0.0 copy-done
  129.9 0.7 copy.21
Async XLA Ops:
  127.7 2.1 %copy-start = (f32[1,256,256]{2,1,0:T(8,128)S(1)}, f32[1,256,256]{2,1,0:T(8,128)}, u32[]{:S(2)}) copy-start(f32[1,256,256]{2,1,0:T(8,128)} %get-tuple-element.8) | copy-start | bytes 786436

commit v3 on v2

--- a/solution.py
+++ b/solution.py
@@ -18,6 +18,7 @@
 
 NG, ND = 4, 32
 NF = NG * ND
+CHIPS = NF // 2
 NY, NZ = 256, 256
 XS, YS = 32, 8
 HALO = MECH_SWEEPS + 1
@@ -25,6 +26,8 @@
 XW = CH * SL
 YW = 3 * YS
 BLOCKS = 4
+PARTS = 2
+PR = NY // PARTS
 
 ALPHA = 1.0 - RELAX * 27.0 / 26.0
 BETA = RELAX / 26.0
@@ -63,10 +66,10 @@
     p0_h, sc_h, st_h, tx_h, ty_h, tz_h, u_h, mod_h, cell_h, well_h, cnt_h, idx_h, rate_h,
     p_out, u_out, s_out,
     cell_ref, well_ref, cnt_ref, idx_ref, rate_ref,
-    press, base, east, west, north, south, upper, lower, rdiag, wells, halo_lo, halo_hi,
-    msg, ag0, ag, masks,
+    press, field, base, east, west, north, south, upper, lower, rdiag, wells, sinks, near,
+    halo_lo, halo_hi, col_hot, near_msg, near_lo, near_hi, msg, other, joint, ag0, ag, masks,
     ppad, nat, pwin, ua, ub, gain, force, xsum, shear, dy_z, dz_z, dx_z, betas, strain,
-    small_sem, load_sem, uload_sem, halo_send, halo_recv, tx_send, tx_recv, ag_send, ag_recv,
+    small_sem, load_sem, uload_sem, halo_send, halo_recv, tx_send, tx_recv, near_send, near_recv, join_send, join_recv, ag_send, ag_recv,
     usend, urecv, xsend, xrecv, relay_sem, pw_send, pw_recv, pw_self, st_send, st_recv, st_self,
     out_sem,
 ):
@@ -143,22 +146,41 @@
 
     barrier = pltpu.get_barrier_semaphore()
 
-    def greet(i, carry):
-        pl.semaphore_signal(
-            barrier, inc=1, device_id=flow_dev(lax.rem(f + i, NF)), device_id_type=MESH
-        )
-        return carry
-
-    lax.fori_loop(1, NF, greet, 0)
+    core, z_lo = lax.rem(g, 2), g // 2
+    z_hi, phys_x, phys_y = d // 16, lax.rem(d // 4, 4), lax.rem(d, 4)
+    phys_z = 2 * z_hi + z_lo
+    spots = sorted(
+        ((x, y) for x in range(4) for y in range(4)),
+        key=lambda o: -(min(o[0], 4 - o[0]) + min(o[1], 4 - o[1])),
+    )
+    for ox, oy in spots:
+        x, y = lax.rem(phys_x + ox, 4), lax.rem(phys_y + oy, 4)
+
+        def greet(j, carry, x=x, y=y):
+            z = lax.rem(phys_z + lax.rem(2 + 3 * (j // 2), 4), 4)
+            c = lax.rem(core + 1 + lax.rem(j, 2), 2)
+            pl.semaphore_signal(
+                barrier, inc=1, device_id=(lax.rem(z, 2) * 2 + c, (z // 2) * 16 + x * 4 + y),
+                device_id_type=MESH,
+            )
+            return carry
+
+        if ox == 0 and oy == 0:
+            lax.fori_loop(0, 5, greet, 0)
+            lax.fori_loop(6, 8, greet, 0)
+        else:
+            lax.fori_loop(0, 8, greet, 0)
 
     @pl.when(first)
     def _():
         halo_lo[...] = jnp.zeros(halo_lo.shape, F32)
+        near_lo[...] = jnp.zeros(near_lo.shape, F32)
         west[...] = jnp.zeros((NY, NZ), F32)
 
     @pl.when(last)
     def _():
         halo_hi[...] = jnp.zeros(halo_hi.shape, F32)
+        near_hi[...] = jnp.zeros(near_hi.shape, F32)
 
     ppad[0:YS, :] = jnp.zeros((YS, NZ), F32)
     ppad[NY + YS :, :] = jnp.zeros((YS, NZ), F32)
@@ -169,127 +191,158 @@
     for c in small_loads:
         c.wait()
     lane = iota((1, 128), 1)
-    weight_sums = []
-    for b in range(BLOCKS):
-        live = lane < cnt_ref[b]
-        weight = jnp.where(live, idx_ref[b : b + 1, :], 0.0)
-        cell = cell_ref[b : b + 1, :]
-        row, col = cell // NZ, lax.rem(cell, NZ)
-        at_row = iota((NY, 128), 0) == row
-        at_col = jnp.where(iota((NZ, 128), 0) == col, 1.0, 0.0).astype(jnp.bfloat16)
-        rest = weight
+
+    def hot(shape, index):
+        return jnp.where(iota(shape, 0) == index, 1.0, 0.0).astype(jnp.bfloat16)
+
+    def thirds(v):
+        out = []
+        for _ in range(3):
+            part = v.astype(jnp.bfloat16)
+            v = v - part.astype(F32)
+            out.append(part)
+        return out
+
+    def dense(cell, value):
+        at_row = iota((NY, 128), 0) == cell // NZ
+        at_col = hot((NZ, 128), lax.rem(cell, NZ))
         plane = jnp.zeros((NY, NZ), F32)
-        for _ in range(3):
-            part = rest.astype(jnp.bfloat16)
-            rest = rest - part.astype(F32)
+        for part in thirds(value):
             spread = jnp.where(at_row, part.astype(F32), 0.0).astype(jnp.bfloat16)
             plane = plane + lax.dot_general(
                 spread, at_col, (((1,), (1,)), ((), ())), preferred_element_type=F32
             )
-        wells[b] = plane
-        weight_sums.append(jnp.sum(weight, axis=1, keepdims=True))
+        return plane
+
+    weights = []
+    for b in range(BLOCKS):
+        weight = jnp.where(lane < cnt_ref[b], idx_ref[b : b + 1, :], 0.0)
+        cell = cell_ref[b : b + 1, :]
+        wells[b] = dense(cell, weight)
+        col_hot[:, b * 128 : (b + 1) * 128] = hot((NZ, 128), lax.rem(cell, NZ))
+        near_msg[b : b + 1, :] = cell.astype(F32)
+        weights.append(weight)
+    weight_sums = [jnp.sum(w, axis=1, keepdims=True) for w in weights]
 
     for c in plane_loads:
         c.wait()
 
-    def halo_copies(k):
-        up = pltpu.make_async_remote_copy(
-            press.at[k], halo_lo.at[k], halo_send.at[0, k], halo_recv.at[0, k],
-            device_id=after, device_id_type=MESH,
-        )
-        down = pltpu.make_async_remote_copy(
-            press.at[k], halo_hi.at[k], halo_send.at[1, k], halo_recv.at[1, k],
-            device_id=before, device_id_type=MESH,
-        )
-        return up, down
+    def start_pair(copies, to_up, to_down):
+        @pl.when(to_up)
+        def _():
+            copies[0].start()
+
+        @pl.when(to_down)
+        def _():
+            copies[1].start()
+
+    def recv_pair(copies, to_up, to_down):
+        @pl.when(to_down)
+        def _():
+            copies[0].wait_recv()
+
+        @pl.when(to_up)
+        def _():
+            copies[1].wait_recv()
+
+    def send_pair(copies, to_up, to_down):
+        @pl.when(to_up)
+        def _():
+            copies[0].wait_send()
+
+        @pl.when(to_down)
+        def _():
+            copies[1].wait_send()
+
+    def halo_copies(k, j):
+        part = pl.ds(j * PR, PR)
+        return [
+            pltpu.make_async_remote_copy(
+                press.at[k, part], buffer.at[k, part], halo_send.at[s, k, j], halo_recv.at[s, k, j],
+                device_id=target, device_id_type=MESH,
+            )
+            for s, (buffer, target) in enumerate([(halo_lo, after), (halo_hi, before)])
+        ]
 
     tx_copy = pltpu.make_async_remote_copy(
         tx_h.at[0], west, tx_send, tx_recv, device_id=after, device_id_type=MESH
     )
-
-    def start_halo(k):
-        up, down = halo_copies(k)
-
-        @pl.when(jnp.logical_not(last))
-        def _():
-            up.start()
-
-        @pl.when(jnp.logical_not(first))
-        def _():
-            down.start()
-
-    def wait_halo(k):
-        up, down = halo_copies(k)
-
-        @pl.when(jnp.logical_not(first))
-        def _():
-            up.wait_recv()
-
-        @pl.when(jnp.logical_not(last))
-        def _():
-            down.wait_recv()
-
-    def wait_halo_send(k):
-        up, down = halo_copies(k)
-
-        @pl.when(jnp.logical_not(last))
-        def _():
-            up.wait_send()
-
-        @pl.when(jnp.logical_not(first))
-        def _():
-            down.wait_send()
+    near_copies = [
+        pltpu.make_async_remote_copy(
+            near_msg, buffer, near_send.at[s], near_recv.at[s], device_id=target, device_id_type=MESH
+        )
+        for s, (buffer, target) in enumerate([(near_lo, after), (near_hi, before)])
+    ]
+    to_after, to_before = jnp.logical_not(last), jnp.logical_not(first)
+
+    chip = z_lo * ND + d
 
     def lanes(values):
         out = jnp.zeros((1, 128), F32)
-        for j, v in enumerate(values):
-            out = jnp.where(lane == j, v, out)
+        for b, v in enumerate(values):
+            out = jnp.where(lane == core * BLOCKS + b, v, out)
         return out
 
     def block_sums(p):
         return lanes([total(wells[b] * p) for b in range(BLOCKS)])
 
-    core, z_lo = lax.rem(g, 2), g // 2
-    z_hi, phys_x, phys_y = d // 16, lax.rem(d // 4, 4), lax.rem(d, 4)
-    spots = sorted(
-        ((x, y) for x in range(4) for y in range(4)),
-        key=lambda o: -(min(o[0], 4 - o[0]) + min(o[1], 4 - o[1])),
-    )
-
-    def gather_refs(k):
-        if k == 0:
-            return msg.at[pl.ds(0, 3), pl.ds(0, 1)], lambda r, n: ag0.at[:, pl.ds(r, n)]
-        return msg.at[2 + k, pl.ds(0, 1)], lambda r, n: ag.at[k - 1, pl.ds(r, n)]
+    def rows_of(ref, k):
+        return ref.at[pl.ds(0, 3), pl.ds(0, 1)] if k == 0 else ref.at[2 + k, pl.ds(0, 1)]
+
+    def gathered(k, r, n):
+        return ag0.at[:, pl.ds(r, n)] if k == 0 else ag.at[k - 1, pl.ds(r, n)]
+
+    def join_copy(k):
+        return pltpu.make_async_remote_copy(
+            rows_of(msg, k), rows_of(other, k), join_send.at[k], join_recv.at[k],
+            device_id=(z_lo * 2 + 1 - core, d), device_id_type=MESH,
+        )
 
     def start_gather(k):
-        src, dst = gather_refs(k)
+        join_copy(k).wait_recv()
+        for j in range(3) if k == 0 else [2 + k]:
+            row = msg[j, 0:1] + other[j, 0:1]
+            joint[j, 0:1] = row
+            if k == 0:
+                ag0[j, pl.ds(chip, 1), :] = row
+            else:
+                ag[k - 1, pl.ds(chip, 1), :] = row
+
+        def send(x, y, oz):
+            z = lax.rem(phys_z + oz, 4)
+            pltpu.make_async_remote_copy(
+                rows_of(joint, k), gathered(k, chip, 1), ag_send.at[k], ag_recv.at[k],
+                device_id=(lax.rem(z, 2) * 2 + core, (z // 2) * 16 + x * 4 + y), device_id_type=MESH,
+            ).start()
+
         for ox, oy in spots:
             x, y = lax.rem(phys_x + ox, 4), lax.rem(phys_y + oy, 4)
-
-            def send(i, carry, x=x, y=y):
-                j = 7 - i
-                zh = lax.rem(z_hi + j // 4, 2)
-                zl = lax.rem(z_lo + lax.rem(j // 2, 2), 2)
-                c = lax.rem(core + lax.rem(j, 2), 2)
-                pltpu.make_async_remote_copy(
-                    src, dst(f, 1), ag_send.at[k], ag_recv.at[k],
-                    device_id=(zl * 2 + c, zh * 16 + x * 4 + y), device_id_type=MESH,
-                ).start()
-                return carry
-
-            lax.fori_loop(0, 7 if ox == 0 and oy == 0 else 8, send, 0)
+            if ox == 0 and oy == 0:
+                for oz in (2, 1, 3):
+                    send(x, y, oz)
+            else:
+
+                def step(j, carry, x=x, y=y):
+                    send(x, y, lax.rem(2 + 3 * j, 4))
+                    return carry
+
+                lax.fori_loop(0, 4, step, 0)
 
     def gather_wait(k, sem):
-        part = gather_refs(k)[1](0, NF - 1)
+        part = gathered(k, 0, CHIPS - 1)
         pltpu.make_async_copy(part, part, sem).wait()
 
-    def y_copies(a):
-        src = mod_h if a == 3 else u_h.at[a]
+    def y_copies(a, first_plane=0, planes=XS):
+        n = HALO - 1 if a == 3 else HALO
         out = []
-        for s, (k, at) in enumerate([(lax.rem(d + 1, ND), 0), (lax.rem(d + ND - 1, ND), 2 * YS)]):
+        for s, (k, at, to) in enumerate(
+            [(lax.rem(d + 1, ND), YS - n, YS - n), (lax.rem(d + ND - 1, ND), 0, 2 * YS)]
+        ):
+            part = pl.ds(first_plane, planes)
+            src = mod_h.at[part, pl.ds(at, n)] if a == 3 else u_h.at[a, part, pl.ds(at, n)]
             out.append(
                 pltpu.make_async_remote_copy(
-                    src, nat.at[a, pl.ds(HALO, XS), pl.ds(at, YS)],
+                    src, nat.at[a, pl.ds(HALO + first_plane, planes), pl.ds(to, n)],
                     usend.at[s, a], urecv.at[s, a], device_id=(g, k), device_id_type=MESH,
                 )
             )
@@ -308,32 +361,14 @@
             )
         return out
 
-    def start_pair(copies, to_up, to_down):
-        @pl.when(to_up)
-        def _():
-            copies[0].start()
-
-        @pl.when(to_down)
-        def _():
-            copies[1].start()
-
-    def recv_pair(copies, to_up, to_down):
-        @pl.when(to_down)
-        def _():
-            copies[0].wait_recv()
-
-        @pl.when(to_up)
-        def _():
-            copies[1].wait_recv()
-
-    def send_pair(copies, to_up, to_down):
-        @pl.when(to_up)
-        def _():
-            copies[0].wait_send()
-
-        @pl.when(to_down)
-        def _():
-            copies[1].wait_send()
+    order = [3, 0, 1, 2]
+    pieces = [(a, j * XS // 4) for a in order for j in range(4)]
+
+    def trickle(n):
+        for _ in range(n):
+            if pieces:
+                a, at = pieces.pop(0)
+                start_pair(y_copies(a, at, XS // 4), has_hi, has_lo)
 
     def pass_on(a):
         recv_pair(y_copies(a), has_hi, has_lo)
@@ -356,19 +391,19 @@
 
     pl.semaphore_wait(barrier, NF - 1)
 
-    @pl.when(jnp.logical_not(last))
+    for j in range(PARTS):
+        start_pair(halo_copies(0, j), to_after, to_before)
+
+    @pl.when(to_after)
     def _():
         tx_copy.start()
 
-    start_halo(0)
     well_ids = [well_ref[b].astype(F32) for b in range(BLOCKS)]
     msg[0, 0:1] = block_sums(press[0])
     msg[1, 0:1] = lanes(weight_sums)
-    msg[2, 0:1] = jnp.where(lane < BLOCKS, lanes(well_ids), -1.0)
-    for j in range(3):
-        ag0[j, pl.ds(f, 1), :] = msg[j, 0:1]
+    msg[2, 0:1] = lanes([w + 1.0 for w in well_ids])
+    join_copy(0).start()
     start_gather(0)
-    start_pair(y_copies(3), has_hi, has_lo)
 
     p0 = press[0]
     storage = rdiag[...]
@@ -385,56 +420,102 @@
     own_u.wait()
     own_m.wait()
 
+    def own_terms(p):
+        acc = base[...] + north[...] * next_y(p) + south[...] * prev_y(p)
+        return acc + upper[...] * pltpu.roll(p, NZ - 1, 1) + lower[...] * pltpu.roll(p, 1, 1)
+
     rates, strengths = [], []
-    for k in range(FLOW_SWEEPS):
-        if k == 0:
-
-            @pl.when(jnp.logical_not(first))
-            def _():
-                tx_copy.wait_recv()
-
-            rdiag[...] = 1.0 / (rdiag[...] + west[...])
-        wait_halo(k)
-        order = [3, 0, 1, 2]
-        pass_on(order[k])
-        if k < 3:
-            start_pair(y_copies(order[k + 1]), has_hi, has_lo)
-        if k > 0:
-            relay(order[k - 1])
-        gather_wait(k, ag_recv.at[k])
-        if k == 0:
-            sums = ag0[0]
-            rate_at = iota((1, 256), 1)
+
+    def find_wells():
+        rate_at = iota((1, 256), 1).astype(F32)
+        for n, (at_g, at_d) in enumerate([(g, d), before, after]):
+            row = (at_g // 2) * ND + at_d
+            first_lane = lax.rem(at_g, 2) * BLOCKS
+            ids = ag0[2, pl.ds(row, 1), :]
             for b in range(BLOCKS):
-                mask = jnp.where(ag0[2] == well_ids[b], 1.0, 0.0)
-                masks[b] = mask
+                well = jnp.sum(jnp.where(lane == first_lane + b, ids, 0.0), axis=1, keepdims=True)
+                mask = jnp.where(ag0[2] == well, 1.0, 0.0)
+                masks[n * BLOCKS + b] = mask
                 strengths.append(total(mask * ag0[1]))
                 rates.append(
                     jnp.sum(
-                        jnp.where(rate_at == well_ref[b], rate_ref[...], 0.0),
-                        axis=1,
-                        keepdims=True,
+                        jnp.where(rate_at == well - 1.0, rate_ref[...], 0.0), axis=1, keepdims=True
                     )
                 )
+
+    def bottoms_of(k, count):
+        sums = ag0[0] if k == 0 else ag[k - 1]
+        return [(rates[n] + total(masks[n] * sums)) / strengths[n] for n in range(count)]
+
+    for k in range(FLOW_SWEEPS + 1):
+        if k == 0:
+            field[...] = own_terms(p0)
+
+            @pl.when(to_before)
+            def _():
+                tx_copy.wait_recv()
+
+            rdiag[...] = 1.0 / (rdiag[...] + west[...])
+            gather_wait(0, ag_recv.at[0])
+            find_wells()
+            bottoms = bottoms_of(0, BLOCKS)
+            inflow = wells[0] * bottoms[0]
+            for b in range(1, BLOCKS):
+                inflow = inflow + wells[b] * bottoms[b]
+            field[...] += inflow
+        elif k == 1:
+            p = press[1]
         else:
-            sums = ag[k - 1]
-        bottoms = [(rates[b] + total(masks[b] * sums)) / strengths[b] for b in range(BLOCKS)]
-        p = press[k]
-        acc = base[...] + east[...] * halo_hi[k] + west[...] * halo_lo[k]
-        acc = acc + north[...] * next_y(p) + south[...] * prev_y(p)
-        acc = acc + upper[...] * pltpu.roll(p, NZ - 1, 1) + lower[...] * pltpu.roll(p, 1, 1)
-        for b in range(BLOCKS):
-            acc = acc + wells[b] * bottoms[b]
-        new = acc * rdiag[...]
-        if k < FLOW_SWEEPS - 1:
-            press[k + 1] = new
-            start_halo(k + 1)
-            row = block_sums(new)
-            msg[3 + k, 0:1] = row
-            ag[k, pl.ds(f, 1), :] = row
-            start_gather(k + 1)
-        else:
-            ppad[YS : YS + NY, :] = new
+            gather_wait(k - 1, ag_recv.at[k - 1])
+            bottoms = bottoms_of(k - 1, 3 * BLOCKS if k < FLOW_SWEEPS else BLOCKS)
+            p = press[k]
+            for b in range(BLOCKS):
+                p = p + sinks[b] * bottoms[b]
+        if k == FLOW_SWEEPS:
+            ppad[YS : YS + NY, :] = p
+            break
+        if k > 0:
+            msg[2 + k, 0:1] = block_sums(p)
+            join_copy(k).start()
+            field[...] = own_terms(p)
+            start_gather(k)
+        if k > 1:
+            from_lo = near[0] * bottoms[BLOCKS]
+            from_hi = near[BLOCKS] * bottoms[2 * BLOCKS]
+            for b in range(1, BLOCKS):
+                from_lo = from_lo + near[b] * bottoms[BLOCKS + b]
+                from_hi = from_hi + near[BLOCKS + b] * bottoms[2 * BLOCKS + b]
+            field[...] += east[...] * from_hi + west[...] * from_lo
+        for j in range(PARTS):
+            send_pair(halo_copies(k, j), to_after, to_before)
+        trickle(4)
+        for j in range(PARTS):
+            part = slice(j * PR, (j + 1) * PR)
+            recv_pair(halo_copies(k, j), to_after, to_before)
+            acc = field[part] + east[part] * halo_hi[k, part] + west[part] * halo_lo[k, part]
+            press[k + 1, part] = acc * rdiag[part]
+            if k < FLOW_SWEEPS - 1:
+                start_pair(halo_copies(k + 1, j), to_after, to_before)
+        if k == 0:
+            found = jnp.zeros((NY, BLOCKS * 128), F32)
+            for third in thirds(rdiag[...]):
+                found = found + jnp.dot(third, col_hot[...], preferred_element_type=F32)
+            for b in range(BLOCKS):
+                at_row = iota((NY, 128), 0) == cell_ref[b : b + 1, :] // NZ
+                at_cell = jnp.where(at_row, found[:, b * 128 : (b + 1) * 128], 0.0)
+                at_cell = jnp.sum(at_cell, axis=0, keepdims=True)
+                near_msg[BLOCKS + b : BLOCKS + b + 1, :] = weights[b] * at_cell
+                sinks[b] = wells[b] * rdiag[...]
+            start_pair(near_copies, to_after, to_before)
+        if k == 1:
+            recv_pair(near_copies, to_after, to_before)
+            for s, buffer in enumerate([near_lo, near_hi]):
+                for b in range(BLOCKS):
+                    near[s * BLOCKS + b] = dense(
+                        buffer[b : b + 1, :].astype(jnp.int32), buffer[BLOCKS + b : BLOCKS + b + 1, :]
+                    )
+        if k > 0:
+            pass_on(order[k - 1])
 
     def window(t):
         return ppad.at[pl.ds(pl.multiple_of(t * YS, YS), YW)]
@@ -475,7 +556,8 @@
         part = nat.at[0, pl.ds(0, count)]
         pltpu.make_async_copy(part, part, sem).wait()
 
-    relay(2)
+    relay(order[0])
+    pass_on(order[3])
     for c in relay_copies(3):
         c.wait()
 
@@ -488,9 +570,31 @@
         return carry
 
     lax.fori_loop(2, YW - 2, gain_row, 0)
+    for a in order[1:]:
+        relay(a)
     for a in range(3):
         for c in relay_copies(a):
             c.wait()
+
+    @pl.when(jnp.logical_not(last))
+    def _():
+        tx_copy.wait_send()
+
+    for k in range(FLOW_SWEEPS):
+        gather_wait(k, ag_send.at[k])
+        join_copy(k).wait_send()
+    send_pair(near_copies, to_after, to_before)
+    for a in range(4):
+        send_pair(y_copies(a), has_hi, has_lo)
+    window_wait(ND - 1, pw_send.at[0])
+
+    @pl.when(to_hi)
+    def _():
+        window_wait(ND, pw_send.at[1])
+
+    @pl.when(to_lo)
+    def _():
+        window_wait(ND, pw_send.at[2])
 
     own_window.wait()
     window_wait(ND - 1, pw_recv.at[0])
@@ -514,9 +618,8 @@
 
     lax.fori_loop(2, YW - 2, force_row, 0)
 
-    for s in range(MECH_SWEEPS):
+    def sweep_tools(s):
         src, dst = (ua, ub) if s % 2 == 0 else (ub, ua)
-        y0, y1 = 2 + s, YW - 2 - s
 
         def row_values(y, src=src):
             tz, dz = [], []
@@ -568,17 +671,31 @@
                     r = box + COUPLE * mixed[c] + (ALPHA / BETA) * src[c, i, y]
                     dst[c, i, y] = beta * r + force[c, i, y]
 
-        for y in (y0 - 1, y0, y0 + 1):
-            row_store(y, row_values(y))
-
-        def mech_row(y, carry, y1=y1):
-            ahead = jnp.minimum(y + 2, y1)
-            values = row_values(ahead)
+        return row_values, row_store, combine
+
+    def first_rows(s, row_values):
+        return [(y, row_values(y)) for y in (1 + s, 2 + s, 3 + s)]
+
+    tools = [sweep_tools(s) for s in range(MECH_SWEEPS)]
+    for y, values in first_rows(0, tools[0][0]):
+        tools[0][1](y, values)
+    for s, (row_values, row_store, combine) in enumerate(tools):
+        y0, y1 = 2 + s, YW - 2 - s
+
+        def mech_row(y, carry, row_values=row_values, row_store=row_store, combine=combine):
+            values = row_values(y + 2)
             combine(y)
-            row_store(ahead, values)
+            row_store(y + 2, values)
             return carry
 
-        lax.fori_loop(y0, y1, mech_row, 0, unroll=2)
+        lax.fori_loop(y0, y1 - 2, mech_row, 0, unroll=2)
+        values = row_values(y1)
+        combine(y1 - 2)
+        row_store(y1, values)
+        ahead = first_rows(s + 1, tools[s + 1][0]) if s < MECH_SWEEPS - 1 else []
+        combine(y1 - 1)
+        for y, values in ahead:
+            row_store(y, values)
 
     final = ua if MECH_SWEEPS % 2 == 0 else ub
 
@@ -622,25 +739,6 @@
     for c in u_copies:
         c.start()
 
-    @pl.when(jnp.logical_not(last))
-    def _():
-        tx_copy.wait_send()
-
-    for k in range(FLOW_SWEEPS):
-        wait_halo_send(k)
-        gather_wait(k, ag_send.at[k])
-    for a in range(4):
-        send_pair(y_copies(a), has_hi, has_lo)
-    window_wait(ND - 1, pw_send.at[0])
-
-    @pl.when(to_hi)
-    def _():
-        window_wait(ND, pw_send.at[1])
-
-    @pl.when(to_lo)
-    def _():
-        window_wait(ND, pw_send.at[2])
-
     p_copy.wait()
     for c in u_copies:
         c.wait()
@@ -648,6 +746,28 @@
     part = ppad.at[pl.ds(0, (ND - 1) * YS)]
     pltpu.make_async_copy(part, part, st_send).wait()
     pltpu.make_async_copy(part, part, st_recv).wait()
+
+
+def hand_over(p_in, u_in, s_in, p_out, u_out, s_out, p_buf, u_buf, s_buf, sem_in, sem_out):
+    pairs = []
+    half = NY // 2
+    for src, buf, dst in [(p_in, p_buf, p_out), (s_in, s_buf, s_out)]:
+        for j in range(2):
+            part = pl.ds(j * half, half)
+            pairs.append((src.at[0, part], buf.at[0, part], dst.at[0, part]))
+    for c in range(3):
+        for j in range(2):
+            part = pl.ds(j * XS // 2, XS // 2)
+            pairs.append((u_in.at[c, part], u_buf.at[c, part], u_out.at[c, part]))
+    loads = [pltpu.make_async_copy(a, b, sem_in.at[i]) for i, (a, b, _) in enumerate(pairs)]
+    saves = [pltpu.make_async_copy(b, c, sem_out.at[i]) for i, (_, b, c) in enumerate(pairs)]
+    for c in loads:
+        c.start()
+    for c, s in zip(loads, saves):
+        c.wait()
+        s.start()
+    for s in saves:
+        s.wait()
 
 
 def body(
@@ -659,14 +779,15 @@
     plane = (NY, NZ)
     slabs = (SL, YW, CH, NZ)
     hbm = pl.BlockSpec(memory_space=pl.ANY)
-    return pl.pallas_call(
+    shapes = (
+        jax.ShapeDtypeStruct((1, NY, NZ), F32),
+        jax.ShapeDtypeStruct((3, XS, YS, NZ), F32),
+        jax.ShapeDtypeStruct((1, NY, NZ), F32),
+    )
+    results = pl.pallas_call(
         kernel,
         name="poro_step",
-        out_shape=(
-            jax.ShapeDtypeStruct((1, NY, NZ), F32),
-            jax.ShapeDtypeStruct((3, XS, YS, NZ), F32),
-            jax.ShapeDtypeStruct((1, NY, NZ), F32),
-        ),
+        out_shape=shapes,
         in_specs=[hbm] * 13,
         out_specs=(hbm, hbm, hbm),
         scratch_shapes=[
@@ -675,7 +796,8 @@
             pltpu.SMEM((BLOCKS,), jnp.int32),
             vmem(BLOCKS, 128),
             vmem(1, 256),
-            vmem(FLOW_SWEEPS, *plane),
+            vmem(FLOW_SWEEPS + 1, *plane),
+            vmem(*plane),
             vmem(*plane),
             vmem(*plane),
             vmem(*plane),
@@ -685,12 +807,20 @@
             vmem(*plane),
             vmem(*plane),
             vmem(BLOCKS, *plane),
+            vmem(BLOCKS, *plane),
+            vmem(2 * BLOCKS, *plane),
             vmem(FLOW_SWEEPS, *plane),
             vmem(FLOW_SWEEPS, *plane),
+            pltpu.VMEM((NZ, BLOCKS * 128), jnp.bfloat16),
+            vmem(2 * BLOCKS, 128),
+            vmem(2 * BLOCKS, 128),
+            vmem(2 * BLOCKS, 128),
             vmem(3 + FLOW_SWEEPS - 1, 8, 128),
-            vmem(3, NF, 128),
-            vmem(FLOW_SWEEPS - 1, NF, 128),
-            vmem(BLOCKS, NF, 128),
+            vmem(3 + FLOW_SWEEPS - 1, 8, 128),
+            vmem(3 + FLOW_SWEEPS - 1, 8, 128),
+            vmem(3, CHIPS, 128),
+            vmem(FLOW_SWEEPS - 1, CHIPS, 128),
+            vmem(3 * BLOCKS, CHIPS, 128),
             vmem(NY + 2 * YS, NZ),
             vmem(4, XW, YW, NZ),
             vmem(*slabs),
@@ -708,10 +838,14 @@
             dma((5,)),
             dma((6,)),
             dma((2,)),
-            dma((2, FLOW_SWEEPS)),
-            dma((2, FLOW_SWEEPS)),
+            dma((2, FLOW_SWEEPS, PARTS)),
+            dma((2, FLOW_SWEEPS, PARTS)),
             dma,
             dma,
+            dma((2,)),
+            dma((2,)),
+            dma((FLOW_SWEEPS,)),
+            dma((FLOW_SWEEPS,)),
             dma((FLOW_SWEEPS,)),
             dma((FLOW_SWEEPS,)),
             dma((2, 4)),
@@ -735,6 +869,20 @@
         perf_cell, perf_well, perf_count, perf_index,
         well_rate.reshape(1, -1),
     )
+    return pl.pallas_call(
+        hand_over,
+        name="hand_over",
+        out_shape=shapes,
+        in_specs=[hbm] * 3,
+        out_specs=(hbm, hbm, hbm),
+        scratch_shapes=[
+            vmem(1, NY, NZ),
+            vmem(3, XS, YS, NZ),
+            vmem(1, NY, NZ),
+            dma((10,)),
+            dma((10,)),
+        ],
+    )(*results)
 
 
 def solution(mesh):

time: 131 us -> 120 us (0.916)
  Pallas kernels: 125 us -> 119 us
  local copies, waits for them, and re-layouts: 4.48 us -> 0 us
    pallas_call x1 -> x2, Pallas kernels: 125 us -> 119 us  [the longest x1 117 us: body(): pl.pallas_call(kernel, name='poro_step', out_shape=shapes, in_specs=[hbm]...]
    unnamed x5 -> x0, local copies, waits for them, and re-layouts: 4.48 us -> none
where the time goes in v3:
time: 120 us
  Pallas kernels  119 us (99%)
    pallas_call x1, Pallas kernels, body(): pl.pallas_call(kernel, name='poro_step', out_shape=shapes, in_specs=[hbm]...  117 us

profile of v3, /device:TPU:1, one launch (start us, length us, event | category | flops | bytes accessed | tf_op | source)
XLA Modules:
  0.0 120.2 jit_solution(4696817111886858407)
XLA Ops:
  0.6 117.2 %poro_step.1 = (f32[1,256,256]{2,1,0:T(8,128)}, f32[3,32,8,256]{3,2,1,0:T(8,128)}, f32[1,256,256]{2,1,0:T(8,128)}) custom-call(f32[1,256,256]{2,1,0:T(8,128)} %p0_h.1, f32[1,256,256]{2,1,0:T(8,128)} %sc_h.1, f32[1,256,256]{2,1,0:T(8,128)} %st_h.1, f32[1,256,256]{2,1,0:T(8,128)} %tx_h.1, f32[1,256,256]{2,1,0:T(8,128)} %ty_h.1, f32[1,256,256]{2,1,0:T(8,128)} %tz_h.1, ...), custom_call_target="tpu_custom_call" | custom-call | tf_op jit(solution)/shard_map/poro_step/pallas_call | solution.py:787
  117.8 2.2 %hand_over.1 = (f32[1,256,256]{2,1,0:T(8,128)}, f32[3,32,8,256]{3,2,1,0:T(8,128)}, f32[1,256,256]{2,1,0:T(8,128)}) custom-call(f32[1,256,256]{2,1,0:T(8,128)} %get-tuple-element.6.p_in, f32[3,32,8,256]{3,2,1,0:T(8,128)} %get-tuple-element.7.u_in, f32[1,256,256]{2,1,0:T(8,128)} %get-tuple-element.8.s_in), custom_call_target="tpu_custom_call" | custom-call | tf_op jit(solution)/shard_map/hand_over/pallas_call | solution.py:872

commit v4 on v3

--- a/solution.py
+++ b/solution.py
@@ -488,7 +488,7 @@
             field[...] += east[...] * from_hi + west[...] * from_lo
         for j in range(PARTS):
             send_pair(halo_copies(k, j), to_after, to_before)
-        trickle(4)
+        trickle([0, 4, 4, 4][k])
         for j in range(PARTS):
             part = slice(j * PR, (j + 1) * PR)
             recv_pair(halo_copies(k, j), to_after, to_before)
@@ -514,8 +514,6 @@
                     near[s * BLOCKS + b] = dense(
                         buffer[b : b + 1, :].astype(jnp.int32), buffer[BLOCKS + b : BLOCKS + b + 1, :]
                     )
-        if k > 0:
-            pass_on(order[k - 1])
 
     def window(t):
         return ppad.at[pl.ds(pl.multiple_of(t * YS, YS), YW)]
@@ -551,13 +549,17 @@
 
     p_copy = pltpu.make_async_copy(ppad.at[pl.ds(YS, NY)], p_out.at[0], out_sem.at[0])
     p_copy.start()
+    trickle(16)
 
     def window_wait(count, sem):
         part = nat.at[0, pl.ds(0, count)]
         pltpu.make_async_copy(part, part, sem).wait()
 
+    pass_on(order[0])
+    pass_on(order[1])
+    pass_on(order[2])
     relay(order[0])
-    pass_on(order[3])
+    relay(order[1])
     for c in relay_copies(3):
         c.wait()
 
@@ -570,8 +572,9 @@
         return carry
 
     lax.fori_loop(2, YW - 2, gain_row, 0)
-    for a in order[1:]:
-        relay(a)
+    pass_on(order[3])
+    relay(order[2])
+    relay(order[3])
     for a in range(3):
         for c in relay_copies(a):
             c.wait()

time: 120 us -> 118 us (0.983)
  Pallas kernels: 119 us -> 117 us
    pallas_call x1, Pallas kernels: 117 us -> 115 us  [body(): pl.pallas_call(kernel, name='poro_step', out_shape=shapes, in_specs=[hbm]...]
where the time goes in v4:
time: 118 us
  Pallas kernels  117 us (99%)
    pallas_call x1, Pallas kernels, body(): pl.pallas_call(kernel, name='poro_step', out_shape=shapes, in_specs=[hbm]...  115 us

profile of v4, /device:TPU:1, one launch (start us, length us, event | category | flops | bytes accessed | tf_op | source)
XLA Modules:
  0.0 117.9 jit_solution(8262329162852636843)
XLA Ops:
  0.6 114.9 %poro_step.1 = (f32[1,256,256]{2,1,0:T(8,128)}, f32[3,32,8,256]{3,2,1,0:T(8,128)}, f32[1,256,256]{2,1,0:T(8,128)}) custom-call(f32[1,256,256]{2,1,0:T(8,128)} %p0_h.1, f32[1,256,256]{2,1,0:T(8,128)} %sc_h.1, f32[1,256,256]{2,1,0:T(8,128)} %st_h.1, f32[1,256,256]{2,1,0:T(8,128)} %tx_h.1, f32[1,256,256]{2,1,0:T(8,128)} %ty_h.1, f32[1,256,256]{2,1,0:T(8,128)} %tz_h.1, ...), custom_call_target="tpu_custom_call" | custom-call | tf_op jit(solution)/shard_map/poro_step/pallas_call | solution.py:790
  115.6 2.2 %hand_over.1 = (f32[1,256,256]{2,1,0:T(8,128)}, f32[3,32,8,256]{3,2,1,0:T(8,128)}, f32[1,256,256]{2,1,0:T(8,128)}) custom-call(f32[1,256,256]{2,1,0:T(8,128)} %get-tuple-element.6.p_in, f32[3,32,8,256]{3,2,1,0:T(8,128)} %get-tuple-element.7.u_in, f32[1,256,256]{2,1,0:T(8,128)} %get-tuple-element.8.s_in), custom_call_target="tpu_custom_call" | custom-call | tf_op jit(solution)/shard_map/hand_over/pallas_call | solution.py:875

commit v5 on v4

--- a/solution.py
+++ b/solution.py
@@ -362,13 +362,13 @@
         return out
 
     order = [3, 0, 1, 2]
-    pieces = [(a, j * XS // 4) for a in order for j in range(4)]
+    pieces = [(a, j * XS // 2) for a in order for j in range(2)]
 
     def trickle(n):
         for _ in range(n):
             if pieces:
                 a, at = pieces.pop(0)
-                start_pair(y_copies(a, at, XS // 4), has_hi, has_lo)
+                start_pair(y_copies(a, at, XS // 2), has_hi, has_lo)
 
     def pass_on(a):
         recv_pair(y_copies(a), has_hi, has_lo)
@@ -488,7 +488,7 @@
             field[...] += east[...] * from_hi + west[...] * from_lo
         for j in range(PARTS):
             send_pair(halo_copies(k, j), to_after, to_before)
-        trickle([0, 4, 4, 4][k])
+        trickle([0, 2, 2, 2][k])
         for j in range(PARTS):
             part = slice(j * PR, (j + 1) * PR)
             recv_pair(halo_copies(k, j), to_after, to_before)

time: 118 us -> 118 us (level)
  no operation moved by 1% of the time
where the time goes in v5:
time: 118 us
  Pallas kernels  117 us (99%)
    pallas_call x1, Pallas kernels, body(): pl.pallas_call(kernel, name='poro_step', out_shape=shapes, in_specs=[hbm]...  115 us

profile of v5, /device:TPU:1, one launch (start us, length us, event | category | flops | bytes accessed | tf_op | source)
XLA Modules:
  0.0 117.9 jit_solution(3868566903316545056)
XLA Ops:
  0.6 114.9 %poro_step.1 = (f32[1,256,256]{2,1,0:T(8,128)}, f32[3,32,8,256]{3,2,1,0:T(8,128)}, f32[1,256,256]{2,1,0:T(8,128)}) custom-call(f32[1,256,256]{2,1,0:T(8,128)} %p0_h.1, f32[1,256,256]{2,1,0:T(8,128)} %sc_h.1, f32[1,256,256]{2,1,0:T(8,128)} %st_h.1, f32[1,256,256]{2,1,0:T(8,128)} %tx_h.1, f32[1,256,256]{2,1,0:T(8,128)} %ty_h.1, f32[1,256,256]{2,1,0:T(8,128)} %tz_h.1, ...), custom_call_target="tpu_custom_call" | custom-call | tf_op jit(solution)/shard_map/poro_step/pallas_call | solution.py:790
  115.6 2.2 %hand_over.1 = (f32[1,256,256]{2,1,0:T(8,128)}, f32[3,32,8,256]{3,2,1,0:T(8,128)}, f32[1,256,256]{2,1,0:T(8,128)}) custom-call(f32[1,256,256]{2,1,0:T(8,128)} %get-tuple-element.6.p_in, f32[3,32,8,256]{3,2,1,0:T(8,128)} %get-tuple-element.7.u_in, f32[1,256,256]{2,1,0:T(8,128)} %get-tuple-element.8.s_in), custom_call_target="tpu_custom_call" | custom-call | tf_op jit(solution)/shard_map/hand_over/pallas_call | solution.py:875
